TPU v7x, 256 devices: a whole 4x4x8 slice. The times are simulated.
256 devices in a mesh: dp: 64 (over y, z, core), tensor: 4 (over x).
Axes of the slice: x: 4, y: 4, z: 8, core: 2. Of those that a mesh axis runs over, the one named last changes fastest.
Arguments:
- layer_input: bfloat16 [16384, 4096], P(('dp', 'tensor')), may hold values from -6 to 6
- pre_grad: bfloat16 [16384, 5120], P('dp', 'tensor'), may hold values from -6 to 6
- weight_in: bfloat16 [4096, 5120], P(None, 'tensor'), may hold values from -0.09375 to 0.09375
- coeff_prev: float32 [5120, 32], P('tensor'), may hold values from -6 to 6
Outputs:
- input_grad: bfloat16 [16384, 4096], P(('dp', 'tensor'))
- factor_basis: float32 [4096, 32], P('tensor')
- coeff_next: float32 [5120, 32], P('tensor')
All inputs are finite; a program needn't handle non-finite values.
Results may differ from a plain program's by a relative error of at most 0.013.
Values may be sent and summed in bfloat16 or wider, within the bound.
A program may use at most 128 MiB of HBM per device.

v0:
```python
import math

import jax
import jax.numpy as jnp
from jax import lax
from jax.sharding import PartitionSpec as P


def orthonormal(factor, gram_matrix):
    cholesky_factor = jnp.linalg.cholesky(gram_matrix)
    solved = jax.scipy.linalg.solve_triangular(cholesky_factor, factor.T, lower=True)
    return solved.T


def local(layer_input, pre_grad, weight_in, coeff_prev):
    local_rows = pre_grad.shape[0]
    total_rows = local_rows * lax.axis_size("dp")
    loss_scale = 1.0 / math.sqrt(total_rows)
    width = layer_input.shape[1]
    share = width // lax.axis_size("tensor")
    grad_rows = pre_grad
    grad = (
        lax.dot_general(
            lax.all_gather(layer_input, "tensor", axis=0, tiled=True),
            grad_rows,
            (((0,), (0,)), ((), ())),
            preferred_element_type=jnp.float32,
        )
        * loss_scale
    )
    grad_rows = pre_grad
    input_grad = lax.psum_scatter(
        lax.dot_general(
            grad_rows, weight_in, (((1,), (1,)), ((), ())), preferred_element_type=jnp.float32
        ).astype(jnp.bfloat16),
        "tensor",
        scatter_dimension=0,
        tiled=True,
    )
    factor_part = jnp.dot(
        grad, coeff_prev, precision=lax.Precision.HIGHEST, preferred_element_type=jnp.float32
    )
    factor = lax.psum(factor_part, ("dp", "tensor"))
    gram_matrix = jnp.dot(
        factor.T, factor, precision=lax.Precision.HIGHEST, preferred_element_type=jnp.float32
    )
    full_basis = orthonormal(factor, gram_matrix)
    coeff = lax.dot_general(
        grad,
        full_basis,
        (((0,), (0,)), ((), ())),
        precision=lax.Precision.HIGHEST,
        preferred_element_type=jnp.float32,
    )
    own_basis = lax.dynamic_slice_in_dim(full_basis, lax.axis_index("tensor") * share, share, 0)
    coeff_next = lax.psum(coeff, "dp")
    return (input_grad, own_basis, coeff_next)


def solution(mesh):
    return jax.shard_map(
        local,
        mesh=mesh,
        in_specs=(
            P(("dp", "tensor"), None),
            P("dp", "tensor"),
            P(None, "tensor"),
            P("tensor", None),
        ),
        out_specs=(P(("dp", "tensor"), None), P("tensor", None), P("tensor", None)),
        check_vma=False,
    )
```

profile of v0, /device:TPU:1, one launch (start us, length us, event | category | flops | bytes accessed | tf_op | source)
XLA Modules:
  0.0 573.3 jit_solution(13236738841135628388)
XLA Ops:
  7.2 0.0 copy-start
  7.2 0.0 copy-start.2
  7.2 0.0 all-gather.2.cloned.1.call-start
  7.2 0.7 all-gather.2.cloned.1.call-update
  7.9 0.0 all-reduce.3.cloned.1.call-start
  8.0 39.1 %all-gather.2.cloned.1.call-done = bf16[256,4096]{1,0:T(8,128)(2,1)} async-done(((bf16[64,4096]{1,0:T(8,128)(2,1)}), bf16[256,4096]{1,0:T(8,128)(2,1)}) %all-gather.2.cloned.1.call-update) | async-done | bytes 2097168 | tf_op jit(solution)/shard_map/all_gather | solution.py:24
  47.0 0.0 copy-done
  47.0 4.6 fusion.12
  51.6 0.0 copy-start.1
  51.6 7.0 %copy-done.1 = f32[4096,1280]{1,0:T(8,128)} copy-done((f32[4096,1280]{1,0:T(8,128)}, f32[4096,1280]{1,0:T(8,128)S(1)}, u32[]{:S(2)}) %copy-start.1) | copy-done | bytes 20971544
  58.6 0.0 copy-done.2
  58.6 20.0 %fusion.2 = f32[4096,32]{0,1:T(8,128)} fusion(f32[1280,32]{0,1:T(8,128)S(1)} %copy-done.2, f32[4096,1280]{1,0:T(8,128)S(1)} %fusion.12), kind=kOutput, calls=%fused_computation.2 | convolution fusion | flops 2018508800 | bytes 21659648 | tf_op jit(solution)/shard_map/dot_general | solution.py:40
  78.6 0.0 all-reduce.3.cloned.1.call-update
  78.6 0.0 all-reduce.5.cloned.1.call-start
  78.6 250.7 %all-reduce.3.cloned.1.call-done = f32[4096,32]{0,1:T(8,128)} async-done(((f32[4096,32]{0,1:T(8,128)}), f32[4096,32]{0,1:T(8,128)}) %all-reduce.3.cloned.1.call-update) | async-done | bytes 524304 | tf_op jit(solution)/shard_map/psum | solution.py:43
  329.3 1.8 fusion.13
  331.1 0.1 copy.7
  331.2 2.9 cholesky.16
  334.1 0.6 compare_reduce_fusion
  334.8 0.7 fusion.6
  335.4 2.4 custom-call.7
  337.9 1.7 fusion.7
  339.6 15.9 %fusion = f32[1280,32]{0,1:T(8,128)} fusion(f32[32,4096]{1,0:T(8,128)S(1)} %fusion.7, f32[4096,1280]{1,0:T(8,128)} %copy-done.1), kind=kOutput, calls=%fused_computation | convolution fusion | flops 2018508800 | bytes 21659648 | tf_op jit(solution)/shard_map/dot_general | solution.py:48
  355.5 0.0 all-reduce.5.cloned.1.call-update
  355.5 0.0 reduce-scatter.2.cloned.1.call-start
  355.5 12.0 %convolution_convert_fusion = bf16[256,4096]{1,0:T(8,128)(2,1)} fusion(bf16[256,1280]{1,0:T(8,128)(2,1)S(1)} %copy-done, bf16[4096,1280]{1,0:T(8,128)(2,1)} %param.6), kind=kOutput, calls=%fused_computation.6 | convolution fusion | flops 2685403136 | bytes 13238272 | tf_op jit(solution)/shard_map/dot_general | solution.py:33
  367.6 0.0 reduce-scatter.2.cloned.1.call-update
  367.6 0.7 dynamic-slice_bitcast_fusion
  368.3 163.3 %all-reduce.5.cloned.1.call-done = f32[1280,32]{0,1:T(8,128)} async-done(((f32[1280,32]{0,1:T(8,128)}), f32[1280,32]{0,1:T(8,128)}) %all-reduce.5.cloned.1.call-update) | async-done | bytes 163856 | tf_op jit(solution)/shard_map/psum | solution.py:56
  531.6 33.6 %reduce-scatter.2.cloned.1.call-done = bf16[64,4096]{1,0:T(8,128)(2,1)} async-done(((bf16[256,4096]{1,0:T(8,128)(2,1)}), bf16[64,4096]{1,0:T(8,128)(2,1)}) %reduce-scatter.2.cloned.1.call-update) | async-done | bytes 524304 | tf_op jit(solution)/shard_map/reduce_scatter | solution.py:32
  565.2 1.6 copy.10
  (2 shorter events, 0.0 us)
Async XLA Ops:
  7.2 39.9 %copy-start = (bf16[256,1280]{1,0:T(8,128)(2,1)S(1)}, bf16[256,1280]{1,0:T(8,128)(2,1)}, u32[]{:S(2)}) copy-start(bf16[256,1280]{1,0:T(8,128)(2,1)} %param.5) | copy-start | bytes 1966084
  7.2 51.4 %copy-start.2 = (f32[1280,32]{0,1:T(8,128)S(1)}, f32[1280,32]{0,1:T(8,128)}, u32[]{:S(2)}) copy-start(f32[1280,32]{0,1:T(8,128)} %param.7) | copy-start | bytes 491524
  7.2 39.8 %all-gather.2.cloned.1.call-start = ((), (), s32[]{:S(2)}) async-start(), calls=%async_computation.2 | async-start | bytes 2621440 | tf_op jit(solution)/shard_map/all_gather | solution.py:24
  7.9 321.4 %all-reduce.3.cloned.1.call-start = ((), (), s32[]{:S(2)}) async-start(), calls=%async_computation.3 | async-start | bytes 1048576 | tf_op jit(solution)/shard_map/psum | solution.py:43
  51.6 7.0 %copy-start.1 = (f32[4096,1280]{1,0:T(8,128)}, f32[4096,1280]{1,0:T(8,128)S(1)}, u32[]{:S(2)}) copy-start(f32[4096,1280]{1,0:T(8,128)S(1)} %fusion.12) | copy-start | bytes 62914564
  78.6 453.0 %all-reduce.5.cloned.1.call-start = ((), (), s32[]{:S(2)}) async-start(), calls=%async_computation.4 | async-start | bytes 327680 | tf_op jit(solution)/shard_map/psum | solution.py:56
  355.5 209.7 %reduce-scatter.2.cloned.1.call-start = ((), (), s32[]{:S(2)}) async-start(), calls=%async_computation.1 | async-start | bytes 2621440 | tf_op jit(solution)/shard_map/reduce_scatter | solution.py:32
Sparse Core Ops, SparseCore 0:
  9.8 37.1 all-gather.1
  78.7 250.5 all-reduce.2
  355.6 175.9 all-reduce.4
  534.6 30.5 reduce-scatter.1
where the time goes:
time: 574 us; the launch traced here: 573 us
  waiting for transfers between devices  487 us (85%)
  matrix products  55.9 us (10%)
  between operations  13.8 us (2%)
  local copies, waits for them, and re-layouts  9.31 us (2%)
  other arithmetic  6.69 us (1%)
    psum x1, waiting for transfers between devices, local(): factor = lax.psum(factor_part, ('dp', 'tensor'))  251 us
    psum x1, waiting for transfers between devices, local(): coeff_next = lax.psum(coeff, 'dp')  163 us
    all_gather x1, waiting for transfers between devices, local(): lax.all_gather(layer_input, 'tensor', axis=0, tiled=True)  39.1 us
    reduce_scatter x1, waiting for transfers between devices, local(): lax.psum_scatter(lax.dot_general(grad_rows, weight_in, (((1,), (1,)), (()...  33.6 us
    dot_general x1, matrix products, local(): jnp.dot(grad, coeff_prev, precision=lax.Precision.HIGHEST, preferred_elem...  20 us
    dot_general x1, matrix products, local(): lax.dot_general(grad, full_basis, (((0,), (0,)), ((), ())), precision=lax...  15.9 us
    dot_general x1, matrix products, local(): lax.dot_general(grad_rows, weight_in, (((1,), (1,)), ((), ())), preferred...  12 us
  transfers between devices with their start and end apart: 4, of which 4 were waited for; matrix products, arithmetic and copies ran while one was open for 2% of the time, Pallas kernels for 0%

commit v1 on v0

v1 whole, which is shorter than its diff:
```python
import functools
import math

import jax
import jax.numpy as jnp
from jax import lax
from jax.experimental import pallas as pl
from jax.experimental.pallas import tpu as pltpu
from jax.sharding import PartitionSpec as P

MESH = pl.DeviceIdType.MESH
HIGH = lax.Precision.HIGHEST
F32 = jnp.float32
BF16 = jnp.bfloat16
NN = (((1,), (0,)), ((), ()))
NT = (((1,), (1,)), ((), ()))
R = 32
NY, NZ = 4, 8


def split3(a):
    hi = a.astype(BF16)
    rest = a - hi.astype(F32)
    mid = rest.astype(BF16)
    low = (rest - mid.astype(F32)).astype(BF16)
    return jnp.concatenate([hi, mid, low], axis=0)


def fdot(a, b, dims):
    r = lax.dot_general(split3(a), b, dims, preferred_element_type=F32)
    return r[0:R] + r[R : 2 * R] + r[2 * R : 3 * R]


def inverse_cholesky(gram):
    n = gram.shape[0]
    row = lax.broadcasted_iota(jnp.int32, (n, n), 0)
    col = lax.broadcasted_iota(jnp.int32, (n, n), 1)
    eye = jnp.where(row == col, 1.0, 0.0).astype(F32)
    m = jnp.concatenate([gram, eye], axis=1)
    below = lax.broadcasted_iota(jnp.int32, (n, 1), 0)
    diag = jnp.zeros((n, 1), F32)
    for j in range(n):
        pivot = m[j : j + 1, j : j + 1]
        column = m[:, j : j + 1]
        diag = jnp.where(below == j, pivot, diag)
        factor = jnp.where(below > j, column / pivot, 0.0)
        m = m - factor * m[j : j + 1, :]
    return m[:, n : 2 * n] / jnp.sqrt(diag)


def far_offset(j, half):
    return half + lax.div(j + 1, 2) * (1 - 2 * lax.rem(j, 2))


def kernel(
    scale,
    x_ref, g_ref, w_ref, q_ref,
    ig_ref, basis_ref, coeff_ref,
    xv, gv, qv, wv, xs, yr, fp, r2, f3, zr, cp, r4, c3,
    igp, dira, dirb, rela, relb, suma, sumb, fina, finb, igo, bas, cof,
    lsem, wsem, osem, ysem_s, ysem_r, xsem_s, xsem_r, zsem_s, zsem_r,
    rsem, isem_s, isem_r,
):
    d = lax.axis_index("dp")
    t = lax.axis_index("tensor")
    chip = lax.div(d, 2)
    core = lax.rem(d, 2)
    cy, cz = lax.div(chip, NZ), lax.rem(chip, NZ)
    nt = 4
    tok = xv.shape[0]
    share = xs.shape[2]
    half = igp.shape[1] // 2
    left, right, across = lax.rem(t + 3, nt), lax.rem(t + 1, nt), lax.rem(t + 2, nt)

    def other_chips(fn):
        def body(k, carry):
            qy = lax.rem(cy + far_offset(lax.rem(k, NY), NY // 2), NY)
            qz = lax.rem(cz + far_offset(lax.div(k, NY), NZ // 2), NZ)
            fn(qy * NZ + qz)
            return carry

        lax.fori_loop(0, NY * NZ - 1, body, 0)

    loads = [
        pltpu.make_async_copy(q_ref, qv, lsem.at[0]),
        pltpu.make_async_copy(g_ref, gv, lsem.at[1]),
        pltpu.make_async_copy(x_ref, xv, lsem.at[2]),
        pltpu.make_async_copy(
            x_ref.at[:, pl.ds(pl.multiple_of(t * share, share), share)], xs.at[t], lsem.at[3]
        ),
    ]
    for c in loads:
        c.start()
    nb = wsem.shape[0]
    wb = wv.shape[0] // nb

    def w_copy(b):
        rows = pl.ds(pl.multiple_of(b * wb, wb), wb)
        return pltpu.make_async_copy(w_ref.at[rows], wv.at[rows], wsem.at[b])

    for b in range(nb):
        w_copy(b).start()

    bar = pltpu.get_barrier_semaphore()

    def greet(dp, tt):
        pl.semaphore_signal(bar, inc=1, device_id=(dp, tt), device_id_type=MESH)

    def greet_chip(q):
        greet(2 * q, t)
        greet(2 * q + 1, t)

    other_chips(greet_chip)
    greet(2 * chip + 1 - core, t)
    for k in range(1, nt):
        greet(d, lax.rem(t + k, nt))

    loads[0].wait()
    loads[1].wait()
    yr[t] = fdot(qv[...], gv[...], NT)

    def ig_block(b, carry):
        w_copy(b).wait()
        rows = pl.ds(pl.multiple_of(b * wb, wb), wb)
        igp[:, rows] = lax.dot_general(gv[...], wv[rows, :], NT, preferred_element_type=F32).astype(BF16)
        return carry

    lax.fori_loop(0, nb, ig_block, 0)
    loads[2].wait()

    pl.semaphore_wait(bar, 2 * NY * NZ - 1 + nt - 1)

    ycopies, xcopies = [], []
    for k in range(1, nt):
        to = lax.rem(t + k, nt)
        ycopies.append(pltpu.make_async_remote_copy(
            src_ref=yr.at[t], dst_ref=yr.at[t], send_sem=ysem_s.at[k - 1], recv_sem=ysem_r.at[k - 1],
            device_id=(d, to), device_id_type=MESH))
        xcopies.append(pltpu.make_async_remote_copy(
            src_ref=xv.at[:, pl.ds(pl.multiple_of(to * share, share), share)], dst_ref=xs.at[t],
            send_sem=xsem_s.at[k - 1], recv_sem=xsem_r.at[k - 1],
            device_id=(d, to), device_id_type=MESH))
    for c in ycopies:
        c.start()
    for c in xcopies:
        c.start()
    for c in ycopies:
        c.wait_recv()
    yt = (yr[0] + yr[1]) + (yr[2] + yr[3])
    for c in xcopies:
        c.wait_recv()
    loads[3].wait()

    xsl = xs[...].reshape(nt * tok, share)
    part = fdot(yt, xsl, NN) * scale
    ncol = share // 128
    for i in range(R // 8):
        for j in range(ncol):
            fp[i * ncol + j] = part[8 * i : 8 * i + 8, 128 * j : 128 * j + 128]

    def wait_tiles(ref, n, sem):
        view = ref.at[pl.ds(0, n)]
        pltpu.make_async_copy(view, view, sem).wait()

    def tile_copy(src, dst, dp, s, r):
        return pltpu.make_async_remote_copy(
            src_ref=src, dst_ref=dst, send_sem=rsem.at[s], recv_sem=rsem.at[r],
            device_id=(dp, t), device_id_type=MESH)

    def slot(to):
        return lax.rem(d - to + 127, 64)

    other_chips(lambda q: tile_copy(fp.at[q], r2.at[slot(2 * q)], 2 * q, 0, 1).start())

    @pl.when(core == 1)
    def _():
        tile_copy(fp.at[chip], r2.at[slot(2 * chip)], 2 * chip, 0, 1).start()

    def rows_of(o):
        return pl.ds(pl.multiple_of(o * tok, tok), tok)

    def ig_copy(n, src, dst, to):
        return pltpu.make_async_remote_copy(
            src_ref=src, dst_ref=dst, send_sem=isem_s.at[n], recv_sem=isem_r.at[n],
            device_id=(d, to), device_id_type=MESH)

    ca, cb = pl.ds(0, half), pl.ds(half, half)
    c_rela = ig_copy(0, igp.at[rows_of(across), ca], rela, left)
    c_relb = ig_copy(1, igp.at[rows_of(across), cb], relb, right)
    c_dira = ig_copy(2, igp.at[rows_of(right), ca], dira, right)
    c_dirb = ig_copy(3, igp.at[rows_of(left), cb], dirb, left)
    for c in (c_rela, c_relb, c_dira, c_dirb):
        c.start()

    @pl.when(core == 0)
    def _():
        r2[63] = fp[chip]
        wait_tiles(r2, 63, rsem.at[1])
        f3[chip] = jnp.sum(r2[...], axis=0)

        def to_chip(q):
            for c in range(2):
                tile_copy(f3.at[chip], f3.at[chip], 2 * q + c, 2, 3).start()

        other_chips(to_chip)
        tile_copy(f3.at[chip], f3.at[chip], 2 * chip + 1, 2, 3).start()

    c_rela.wait_recv()
    suma[...] = (rela[...].astype(F32) + igp[rows_of(left), ca].astype(F32)).astype(BF16)
    c_fina = ig_copy(4, suma, fina, left)
    c_fina.start()
    c_relb.wait_recv()
    sumb[...] = (relb[...].astype(F32) + igp[rows_of(right), cb].astype(F32)).astype(BF16)
    c_finb = ig_copy(5, sumb, finb, right)
    c_finb.start()

    @pl.when(core == 0)
    def _():
        wait_tiles(f3, 31, rsem.at[3])

    @pl.when(core == 1)
    def _():
        wait_tiles(f3, 32, rsem.at[3])

    ft = jnp.concatenate(
        [jnp.concatenate([f3[i * ncol + j] for j in range(ncol)], axis=1) for i in range(R // 8)], axis=0
    )

    zw = nt * tok
    zr[t, :, 0:zw] = fdot(ft, xsl, NT) * scale
    zr[t, :, zw : zw + R] = lax.dot_general(ft, ft, NT, precision=HIGH, preferred_element_type=F32)
    zcopies = []
    for k in range(1, nt):
        zcopies.append(pltpu.make_async_remote_copy(
            src_ref=zr.at[t], dst_ref=zr.at[t], send_sem=zsem_s.at[k - 1], recv_sem=zsem_r.at[k - 1],
            device_id=(d, lax.rem(t + k, nt)), device_id_type=MESH))
    for c in zcopies:
        c.start()
    for c in zcopies:
        c.wait_recv()
    zt = (zr[0, :, 0:zw] + zr[1, :, 0:zw]) + (zr[2, :, 0:zw] + zr[3, :, 0:zw])
    gs = slice(zw, zw + R)
    gram = (zr[0, :, gs] + zr[1, :, gs]) + (zr[2, :, gs] + zr[3, :, gs])

    cpart = fdot(zt, gv[...], NN)
    ncc = cpart.shape[1] // 128
    nct = R // 8 * ncc
    for i in range(R // 8):
        for j in range(ncc):
            cp[i * ncc + j] = cpart[8 * i : 8 * i + 8, 128 * j : 128 * j + 128]
    other_chips(lambda q: tile_copy(cp.at[q], r4.at[slot(2 * q)], 2 * q, 4, 5).start())

    @pl.when(core == 1)
    def _():
        tile_copy(cp.at[chip], r4.at[slot(2 * chip)], 2 * chip, 4, 5).start()

    @pl.when(core == 0)
    def _():
        r4[63] = cp[chip]

    for e in range(nct - 32):
        to = 8 * e + 1

        @pl.when(d != to)
        def _():
            tile_copy(cp.at[32 + e], r4.at[slot(to)], to, 4, 5).start()

        @pl.when(d == to)
        def _():
            r4[63] = cp[32 + e]

    c_dira.wait_recv()
    c_fina.wait_recv()
    igo[:, ca] = (igp[rows_of(t), ca].astype(F32) + dira[...].astype(F32) + fina[...].astype(F32)).astype(BF16)
    c_dirb.wait_recv()
    c_finb.wait_recv()
    igo[:, cb] = (igp[rows_of(t), cb].astype(F32) + dirb[...].astype(F32) + finb[...].astype(F32)).astype(BF16)
    o_ig = pltpu.make_async_copy(igo, ig_ref, osem.at[0])
    o_ig.start()

    linv = inverse_cholesky(gram)
    bas[...] = lax.dot_general(linv, ft, NN, precision=HIGH, preferred_element_type=F32)
    o_bas = pltpu.make_async_copy(bas, basis_ref, osem.at[1])
    o_bas.start()

    owner = jnp.logical_or(core == 0, lax.rem(chip, 4) == 0)
    mine = chip * (1 - core) + (32 + lax.div(chip, 4)) * core

    @pl.when(owner)
    def _():
        wait_tiles(r4, 63, rsem.at[5])
        c3[mine] = jnp.sum(r4[...], axis=0)

        def to_chip(q):
            for c in range(2):
                tile_copy(c3.at[mine], c3.at[mine], 2 * q + c, 6, 7).start()

        other_chips(to_chip)
        tile_copy(c3.at[mine], c3.at[mine], 2 * chip + 1 - core, 6, 7).start()
        wait_tiles(c3, nct - 1, rsem.at[7])

    @pl.when(jnp.logical_not(owner))
    def _():
        wait_tiles(c3, nct, rsem.at[7])

    ct = jnp.concatenate(
        [jnp.concatenate([c3[i * ncc + j] for j in range(ncc)], axis=1) for i in range(R // 8)], axis=0
    )
    cof[...] = lax.dot_general(linv, ct, NN, precision=HIGH, preferred_element_type=F32)
    o_cof = pltpu.make_async_copy(cof, coeff_ref, osem.at[2])
    o_cof.start()

    for c in ycopies + xcopies + zcopies + [c_rela, c_relb, c_dira, c_dirb, c_fina, c_finb]:
        c.wait_send()

    @pl.when(core == 0)
    def _():
        wait_tiles(r2, 31, rsem.at[0])
        wait_tiles(r2, 63, rsem.at[2])

    @pl.when(core == 1)
    def _():
        wait_tiles(r2, 32, rsem.at[0])

    @pl.when(owner)
    def _():
        wait_tiles(r4, nct - 1, rsem.at[4])
        wait_tiles(r4, 63, rsem.at[6])

    @pl.when(jnp.logical_not(owner))
    def _():
        wait_tiles(r4, nct, rsem.at[4])

    o_ig.wait()
    o_bas.wait()
    o_cof.wait()


def local(layer_input, pre_grad, weight_in, coeff_prev):
    rows = pre_grad.shape[0]
    scale = 1.0 / math.sqrt(rows * lax.axis_size("dp"))
    tok, width = layer_input.shape
    nt = lax.axis_size("tensor")
    hid = pre_grad.shape[1]
    share = width // nt
    half = width // 2
    nb = 8
    dma = pltpu.SemaphoreType.DMA
    vm = pltpu.VMEM
    any_spec = pl.BlockSpec(memory_space=pl.ANY)
    ig, basis, coeff = pl.pallas_call(
        functools.partial(kernel, scale),
        out_shape=(
            jax.ShapeDtypeStruct((tok, width), BF16),
            jax.ShapeDtypeStruct((R, share), F32),
            jax.ShapeDtypeStruct((R, hid), F32),
        ),
        in_specs=[any_spec] * 4,
        out_specs=(any_spec,) * 3,
        scratch_shapes=[
            vm((tok, width), BF16), vm((rows, hid), BF16), vm((R, hid), F32), vm((width, hid), BF16),
            vm((nt, tok, share), BF16), vm((nt, R, rows), F32),
            vm((32, 8, 128), F32), vm((64, 8, 128), F32), vm((32, 8, 128), F32),
            vm((nt, R, rows + 128), F32),
            vm((40, 8, 128), F32), vm((64, 8, 128), F32), vm((40, 8, 128), F32),
            vm((rows, width), BF16),
            *[vm((tok, half), BF16)] * 8,
            vm((tok, width), BF16), vm((R, share), F32), vm((R, hid), F32),
            dma((4,)), dma((nb,)), dma((3,)),
            dma((3,)), dma((3,)), dma((3,)), dma((3,)), dma((3,)), dma((3,)),
            dma((8,)), dma((6,)), dma((6,)),
        ],
        compiler_params=pltpu.CompilerParams(
            collective_id=0, has_side_effects=True, vmem_limit_bytes=48 * 2**20
        ),
    )(layer_input, pre_grad, weight_in, coeff_prev.T)
    return ig, basis.T, coeff.T


def solution(mesh):
    return jax.shard_map(
        local,
        mesh=mesh,
        in_specs=(
            P(("dp", "tensor"), None),
            P("dp", "tensor"),
            P(None, "tensor"),
            P("tensor", None),
        ),
        out_specs=(P(("dp", "tensor"), None), P("tensor", None), P("tensor", None)),
        check_vma=False,
    )
```

time: 574 us -> 65.1 us (0.11)
  waiting for transfers between devices: 487 us -> 0 us
  Pallas kernels: 0 us -> 59.1 us
  matrix products: 55.9 us -> 0 us
  between operations: 13.8 us -> 0.65 us
  other arithmetic: 6.69 us -> 0 us
    psum x2 -> x0, waiting for transfers between devices: 414 us -> none  [the longest x1 251 us: local(): factor = lax.psum(factor_part, ('dp', 'tensor'))]
    pallas_call x0 -> x1, Pallas kernels: none -> 59.1 us  [local(): pl.pallas_call(functools.partial(kernel, scale), out_shape=(jax.ShapeDtyp...]
    dot_general x5 -> x0, matrix products: 54.3 us -> none  [the longest x1 20 us: local(): jnp.dot(grad, coeff_prev, precision=lax.Precision.HIGHEST, preferred_elem...]
    all_gather x1 -> x0, waiting for transfers between devices: 39.1 us -> none  [local(): lax.all_gather(layer_input, 'tensor', axis=0, tiled=True)]
    reduce_scatter x1 -> x0, waiting for transfers between devices: 33.6 us -> none  [local(): lax.psum_scatter(lax.dot_general(grad_rows, weight_in, (((1,), (1,)), (()...]
    another operation x5 -> x0, other arithmetic: 6.68 us -> none  [the longest x3 3.6 us: orthonormal(): cholesky_factor = jnp.linalg.cholesky(gram_matrix)]
  transfers between devices with their start and end apart: 4 -> 0, of which waited for: 4 -> 0; matrix products, arithmetic and copies ran while one was open for 2% -> 0% of each run, Pallas kernels for 0% -> 0%
where the time goes in v1:
time: 65.1 us; the launch traced here: 65 us
  Pallas kernels  59.1 us (91%)
  local copies, waits for them, and re-layouts  5.15 us (8%)
    pallas_call x1, Pallas kernels, local(): pl.pallas_call(functools.partial(kernel, scale), out_shape=(jax.ShapeDtyp...  59.1 us
    unnamed x9, local copies, waits for them, and re-layouts  5.15 us

profile of v1, /device:TPU:1, one launch (start us, length us, event | category | flops | bytes accessed | tf_op | source)
XLA Modules:
  0.0 65.0 jit_solution(7958375603188159491)
XLA Ops:
  0.6 0.0 copy-start
  0.6 1.1 %copy-done = bf16[256,1280]{1,0:T(8,128)(2,1)S(1)} copy-done((bf16[256,1280]{1,0:T(8,128)(2,1)S(1)}, bf16[256,1280]{1,0:T(8,128)(2,1)}, u32[]{:S(2)}) %copy-start) | copy-done | bytes 655384
  1.7 0.0 copy-start.1
  1.7 1.0 %copy-done.1 = bf16[64,4096]{1,0:T(8,128)(2,1)S(1)} copy-done((bf16[64,4096]{1,0:T(8,128)(2,1)S(1)}, bf16[64,4096]{1,0:T(8,128)(2,1)}, u32[]{:S(2)}) %copy-start.1) | copy-done | bytes 524312
  2.8 0.0 copy-start.2
  2.8 0.9 %copy-done.2 = f32[1280,32]{0,1:T(8,128)S(1)} copy-done((f32[1280,32]{0,1:T(8,128)S(1)}, f32[1280,32]{0,1:T(8,128)}, u32[]{:S(2)}) %copy-start.2) | copy-done | bytes 163864
  3.7 59.1 %shard_map.67 = (bf16[64,4096]{1,0:T(8,128)(2,1)S(1)}, f32[32,1024]{1,0:T(8,128)S(1)}, f32[32,1280]{1,0:T(8,128)S(1)}) custom-call(bf16[64,4096]{1,0:T(8,128)(2,1)S(1)} %copy-done.1, bf16[256,1280]{1,0:T(8,128)(2,1)S(1)} %copy-done, bf16[4096,1280]{1,0:T(8,128)(2,1)} %w_ref.1, f32[32,1280]{1,0:T(8,128)S(1)} %bitcast.4), custom_call_target="tpu_custom_call" | custom-call | tf_op jit(solution)/shard_map/pallas_call | solution.py:351
  62.8 0.8 %copy.10 = bf16[64,4096]{1,0:T(8,128)(2,1)} copy(bf16[64,4096]{1,0:T(8,128)(2,1)S(1)} %get-tuple-element.12) | data formatting | bytes 1048576
  63.6 0.7 %copy.11 = f32[1024,32]{0,1:T(8,128)} copy(f32[1024,32]{0,1:T(8,128)S(1)} %bitcast.5) | data formatting | bytes 262144
  64.3 0.7 %copy.12 = f32[1280,32]{0,1:T(8,128)} copy(f32[1280,32]{0,1:T(8,128)S(1)} %bitcast.3) | data formatting | bytes 327680
Async XLA Ops:
  0.6 1.1 %copy-start = (bf16[256,1280]{1,0:T(8,128)(2,1)S(1)}, bf16[256,1280]{1,0:T(8,128)(2,1)}, u32[]{:S(2)}) copy-start(bf16[256,1280]{1,0:T(8,128)(2,1)} %g_ref.1) | copy-start | bytes 1966084
  1.7 1.0 %copy-start.1 = (bf16[64,4096]{1,0:T(8,128)(2,1)S(1)}, bf16[64,4096]{1,0:T(8,128)(2,1)}, u32[]{:S(2)}) copy-start(bf16[64,4096]{1,0:T(8,128)(2,1)} %x_ref.1) | copy-start | bytes 1572868
  2.8 0.9 %copy-start.2 = (f32[1280,32]{0,1:T(8,128)S(1)}, f32[1280,32]{0,1:T(8,128)}, u32[]{:S(2)}) copy-start(f32[1280,32]{0,1:T(8,128)} %param.7) | copy-start | bytes 491524

commit v2 on v1

--- a/solution.py
+++ b/solution.py
@@ -55,10 +55,10 @@
 def kernel(
     scale,
     x_ref, g_ref, w_ref, q_ref,
-    ig_ref, basis_ref, coeff_ref,
+    igo, bas, cof,
     xv, gv, qv, wv, xs, yr, fp, r2, f3, zr, cp, r4, c3,
-    igp, dira, dirb, rela, relb, suma, sumb, fina, finb, igo, bas, cof,
-    lsem, wsem, osem, ysem_s, ysem_r, xsem_s, xsem_r, zsem_s, zsem_r,
+    igp, dira, dirb, rela, relb, suma, sumb, fina, finb,
+    lsem, wsem, ysem_s, ysem_r, xsem_s, xsem_r, zsem_s, zsem_r,
     rsem, isem_s, isem_r,
 ):
     d = lax.axis_index("dp")
@@ -81,6 +81,20 @@
 
         lax.fori_loop(0, NY * NZ - 1, body, 0)
 
+    bar = pltpu.get_barrier_semaphore()
+
+    def greet(dp, tt):
+        pl.semaphore_signal(bar, inc=1, device_id=(dp, tt), device_id_type=MESH)
+
+    def greet_chip(q):
+        greet(2 * q, t)
+        greet(2 * q + 1, t)
+
+    other_chips(greet_chip)
+    greet(2 * chip + 1 - core, t)
+    for k in range(1, nt):
+        greet(d, lax.rem(t + k, nt))
+
     loads = [
         pltpu.make_async_copy(q_ref, qv, lsem.at[0]),
         pltpu.make_async_copy(g_ref, gv, lsem.at[1]),
@@ -101,31 +115,10 @@
     for b in range(nb):
         w_copy(b).start()
 
-    bar = pltpu.get_barrier_semaphore()
-
-    def greet(dp, tt):
-        pl.semaphore_signal(bar, inc=1, device_id=(dp, tt), device_id_type=MESH)
-
-    def greet_chip(q):
-        greet(2 * q, t)
-        greet(2 * q + 1, t)
-
-    other_chips(greet_chip)
-    greet(2 * chip + 1 - core, t)
-    for k in range(1, nt):
-        greet(d, lax.rem(t + k, nt))
-
     loads[0].wait()
     loads[1].wait()
     yr[t] = fdot(qv[...], gv[...], NT)
 
-    def ig_block(b, carry):
-        w_copy(b).wait()
-        rows = pl.ds(pl.multiple_of(b * wb, wb), wb)
-        igp[:, rows] = lax.dot_general(gv[...], wv[rows, :], NT, preferred_element_type=F32).astype(BF16)
-        return carry
-
-    lax.fori_loop(0, nb, ig_block, 0)
     loads[2].wait()
 
     pl.semaphore_wait(bar, 2 * NY * NZ - 1 + nt - 1)
@@ -144,6 +137,15 @@
         c.start()
     for c in xcopies:
         c.start()
+
+    def ig_block(b, carry):
+        w_copy(b).wait()
+        rows = pl.ds(pl.multiple_of(b * wb, wb), wb)
+        igp[:, rows] = lax.dot_general(gv[...], wv[rows, :], NT, preferred_element_type=F32).astype(BF16)
+        return carry
+
+    lax.fori_loop(0, nb, ig_block, 0)
+
     for c in ycopies:
         c.wait_recv()
     yt = (yr[0] + yr[1]) + (yr[2] + yr[3])
@@ -204,15 +206,6 @@
 
         other_chips(to_chip)
         tile_copy(f3.at[chip], f3.at[chip], 2 * chip + 1, 2, 3).start()
-
-    c_rela.wait_recv()
-    suma[...] = (rela[...].astype(F32) + igp[rows_of(left), ca].astype(F32)).astype(BF16)
-    c_fina = ig_copy(4, suma, fina, left)
-    c_fina.start()
-    c_relb.wait_recv()
-    sumb[...] = (relb[...].astype(F32) + igp[rows_of(right), cb].astype(F32)).astype(BF16)
-    c_finb = ig_copy(5, sumb, finb, right)
-    c_finb.start()
 
     @pl.when(core == 0)
     def _():
@@ -269,34 +262,42 @@
         def _():
             r4[63] = cp[32 + e]
 
+    c_rela.wait_recv()
+    suma[...] = (rela[...].astype(F32) + igp[rows_of(left), ca].astype(F32)).astype(BF16)
+    c_fina = ig_copy(4, suma, fina, left)
+    c_fina.start()
+    c_relb.wait_recv()
+    sumb[...] = (relb[...].astype(F32) + igp[rows_of(right), cb].astype(F32)).astype(BF16)
+    c_finb = ig_copy(5, sumb, finb, right)
+    c_finb.start()
+
+    linv = inverse_cholesky(gram)
+    bas[...] = lax.dot_general(linv, ft, NN, precision=HIGH, preferred_element_type=F32)
+
+    owner = jnp.logical_or(core == 0, lax.rem(chip, 4) == 0)
+    mine = chip * (1 - core) + (32 + lax.div(chip, 4)) * core
+
+    @pl.when(owner)
+    def _():
+        wait_tiles(r4, 63, rsem.at[5])
+        c3[mine] = jnp.sum(r4[...], axis=0)
+
+        def to_chip(q):
+            for c in range(2):
+                tile_copy(c3.at[mine], c3.at[mine], 2 * q + c, 6, 7).start()
+
+        other_chips(to_chip)
+        tile_copy(c3.at[mine], c3.at[mine], 2 * chip + 1 - core, 6, 7).start()
+
     c_dira.wait_recv()
     c_fina.wait_recv()
     igo[:, ca] = (igp[rows_of(t), ca].astype(F32) + dira[...].astype(F32) + fina[...].astype(F32)).astype(BF16)
     c_dirb.wait_recv()
     c_finb.wait_recv()
     igo[:, cb] = (igp[rows_of(t), cb].astype(F32) + dirb[...].astype(F32) + finb[...].astype(F32)).astype(BF16)
-    o_ig = pltpu.make_async_copy(igo, ig_ref, osem.at[0])
-    o_ig.start()
-
-    linv = inverse_cholesky(gram)
-    bas[...] = lax.dot_general(linv, ft, NN, precision=HIGH, preferred_element_type=F32)
-    o_bas = pltpu.make_async_copy(bas, basis_ref, osem.at[1])
-    o_bas.start()
-
-    owner = jnp.logical_or(core == 0, lax.rem(chip, 4) == 0)
-    mine = chip * (1 - core) + (32 + lax.div(chip, 4)) * core
 
     @pl.when(owner)
     def _():
-        wait_tiles(r4, 63, rsem.at[5])
-        c3[mine] = jnp.sum(r4[...], axis=0)
-
-        def to_chip(q):
-            for c in range(2):
-                tile_copy(c3.at[mine], c3.at[mine], 2 * q + c, 6, 7).start()
-
-        other_chips(to_chip)
-        tile_copy(c3.at[mine], c3.at[mine], 2 * chip + 1 - core, 6, 7).start()
         wait_tiles(c3, nct - 1, rsem.at[7])
 
     @pl.when(jnp.logical_not(owner))
@@ -307,8 +308,6 @@
         [jnp.concatenate([c3[i * ncc + j] for j in range(ncc)], axis=1) for i in range(R // 8)], axis=0
     )
     cof[...] = lax.dot_general(linv, ct, NN, precision=HIGH, preferred_element_type=F32)
-    o_cof = pltpu.make_async_copy(cof, coeff_ref, osem.at[2])
-    o_cof.start()
 
     for c in ycopies + xcopies + zcopies + [c_rela, c_relb, c_dira, c_dirb, c_fina, c_finb]:
         c.wait_send()
@@ -331,9 +330,13 @@
     def _():
         wait_tiles(r4, nct, rsem.at[4])
 
-    o_ig.wait()
-    o_bas.wait()
-    o_cof.wait()
+
+def write_out(a, b, c, ao, bo, co, sem):
+    copies = [pltpu.make_async_copy(s, o, sem.at[i]) for i, (s, o) in enumerate(((a, ao), (b, bo), (c, co)))]
+    for copy in copies:
+        copy.start()
+    for copy in copies:
+        copy.wait()
 
 
 def local(layer_input, pre_grad, weight_in, coeff_prev):
@@ -348,15 +351,16 @@
     dma = pltpu.SemaphoreType.DMA
     vm = pltpu.VMEM
     any_spec = pl.BlockSpec(memory_space=pl.ANY)
+    vmem_spec = pl.BlockSpec(memory_space=pltpu.VMEM)
     ig, basis, coeff = pl.pallas_call(
         functools.partial(kernel, scale),
         out_shape=(
-            jax.ShapeDtypeStruct((tok, width), BF16),
-            jax.ShapeDtypeStruct((R, share), F32),
-            jax.ShapeDtypeStruct((R, hid), F32),
+            vm((tok, width), BF16),
+            vm((R, share), F32),
+            vm((R, hid), F32),
         ),
         in_specs=[any_spec] * 4,
-        out_specs=(any_spec,) * 3,
+        out_specs=(vmem_spec,) * 3,
         scratch_shapes=[
             vm((tok, width), BF16), vm((rows, hid), BF16), vm((R, hid), F32), vm((width, hid), BF16),
             vm((nt, tok, share), BF16), vm((nt, R, rows), F32),
@@ -365,15 +369,22 @@
             vm((40, 8, 128), F32), vm((64, 8, 128), F32), vm((40, 8, 128), F32),
             vm((rows, width), BF16),
             *[vm((tok, half), BF16)] * 8,
-            vm((tok, width), BF16), vm((R, share), F32), vm((R, hid), F32),
-            dma((4,)), dma((nb,)), dma((3,)),
+            dma((4,)), dma((nb,)),
             dma((3,)), dma((3,)), dma((3,)), dma((3,)), dma((3,)), dma((3,)),
             dma((8,)), dma((6,)), dma((6,)),
         ],
         compiler_params=pltpu.CompilerParams(
-            collective_id=0, has_side_effects=True, vmem_limit_bytes=48 * 2**20
+            collective_id=0, has_side_effects=True, vmem_limit_bytes=60 * 2**20
         ),
     )(layer_input, pre_grad, weight_in, coeff_prev.T)
+    ig, basis, coeff = pl.pallas_call(
+        write_out,
+        out_shape=tuple(jax.ShapeDtypeStruct(v.shape, v.dtype) for v in (ig, basis, coeff)),
+        in_specs=[vmem_spec] * 3,
+        out_specs=(any_spec,) * 3,
+        scratch_shapes=[dma((3,))],
+        compiler_params=pltpu.CompilerParams(vmem_limit_bytes=16 * 2**20),
+    )(ig, basis, coeff)
     return ig, basis.T, coeff.T
 
 

time: 65.1 us -> 56.6 us (0.87)
  local copies, waits for them, and re-layouts: 5.15 us -> 0 us
  Pallas kernels: 59.1 us -> 55.9 us
    unnamed x9 -> x0, local copies, waits for them, and re-layouts: 5.15 us -> none
    pallas_call x1 -> x2, Pallas kernels: 59.1 us -> 55.9 us  [the longest x1 55 us: local(): pl.pallas_call(functools.partial(kernel, scale), out_shape=(vm((tok, widt...]
where the time goes in v2:
time: 56.6 us; the launch traced here: 56.5 us
  Pallas kernels  55.9 us (99%)
  between operations  0.64 us (1%)
    pallas_call x1, Pallas kernels, local(): pl.pallas_call(functools.partial(kernel, scale), out_shape=(vm((tok, widt...  55 us

profile of v2, /device:TPU:1, one launch (start us, length us, event | category | flops | bytes accessed | tf_op | source)
XLA Modules:
  0.0 56.5 jit_solution(1805132839505651588)
XLA Ops:
  0.6 55.0 %shard_map.67 = (bf16[64,4096]{1,0:T(8,128)(2,1)S(1)}, f32[32,1024]{1,0:T(8,128)S(1)}, f32[32,1280]{1,0:T(8,128)S(1)}) custom-call(bf16[64,4096]{1,0:T(8,128)(2,1)} %x_ref.1, bf16[256,1280]{1,0:T(8,128)(2,1)} %g_ref.1, bf16[4096,1280]{1,0:T(8,128)(2,1)} %w_ref.1, f32[32,1280]{1,0:T(8,128)} %bitcast.3), custom_call_target="tpu_custom_call" | custom-call | tf_op jit(solution)/shard_map/pallas_call | solution.py:355
  55.6 0.9 %shard_map.68 = (bf16[64,4096]{1,0:T(8,128)(2,1)}, f32[32,1024]{1,0:T(8,128)}, f32[32,1280]{1,0:T(8,128)}) custom-call(bf16[64,4096]{1,0:T(8,128)(2,1)S(1)} %get-tuple-element.9.a, f32[32,1024]{1,0:T(8,128)S(1)} %get-tuple-element.10.b, f32[32,1280]{1,0:T(8,128)S(1)} %get-tuple-element.11.c), custom_call_target="tpu_custom_call" | custom-call | tf_op jit(solution)/shard_map/pallas_call | solution.py:380

commit v3 on v2

--- a/solution.py
+++ b/solution.py
@@ -59,7 +59,7 @@
     xv, gv, qv, wv, xs, yr, fp, r2, f3, zr, cp, r4, c3,
     igp, dira, dirb, rela, relb, suma, sumb, fina, finb,
     lsem, wsem, ysem_s, ysem_r, xsem_s, xsem_r, zsem_s, zsem_r,
-    rsem, isem_s, isem_r,
+    rsem, isem_s, isem_r, far_sem,
 ):
     d = lax.axis_index("dp")
     t = lax.axis_index("tensor")
@@ -86,12 +86,13 @@
     def greet(dp, tt):
         pl.semaphore_signal(bar, inc=1, device_id=(dp, tt), device_id_type=MESH)
 
-    def greet_chip(q):
-        greet(2 * q, t)
-        greet(2 * q + 1, t)
-
-    other_chips(greet_chip)
-    greet(2 * chip + 1 - core, t)
+    def dp_index(dy, dz, dc):
+        return (lax.rem(cy + dy, NY) * NZ + lax.rem(cz + dz, NZ)) * 2 + (core + dc - 2 * core * dc)
+
+    z_line = [dp_index(0, dz, 0) for dz in (4, 3, 5, 2, 6, 1, 7)]
+    group = [dp_index(dy, 0, dc) for dy in (2, 1, 3, 0) for dc in range(2) if dy or dc]
+    for other in z_line + group:
+        greet(other, t)
     for k in range(1, nt):
         greet(d, lax.rem(t + k, nt))
 
@@ -121,7 +122,7 @@
 
     loads[2].wait()
 
-    pl.semaphore_wait(bar, 2 * NY * NZ - 1 + nt - 1)
+    pl.semaphore_wait(bar, len(z_line) + len(group) + nt - 1)
 
     ycopies, xcopies = [], []
     for k in range(1, nt):
@@ -138,6 +139,9 @@
     for c in xcopies:
         c.start()
 
+    for other in z_line:
+        pl.semaphore_signal(far_sem, inc=1, device_id=(other, t), device_id_type=MESH)
+
     def ig_block(b, carry):
         w_copy(b).wait()
         rows = pl.ds(pl.multiple_of(b * wb, wb), wb)
@@ -172,6 +176,7 @@
     def slot(to):
         return lax.rem(d - to + 127, 64)
 
+    pl.semaphore_wait(far_sem, len(z_line))
     other_chips(lambda q: tile_copy(fp.at[q], r2.at[slot(2 * q)], 2 * q, 0, 1).start())
 
     @pl.when(core == 1)
@@ -282,11 +287,17 @@
         wait_tiles(r4, 63, rsem.at[5])
         c3[mine] = jnp.sum(r4[...], axis=0)
 
-        def to_chip(q):
-            for c in range(2):
-                tile_copy(c3.at[mine], c3.at[mine], 2 * q + c, 6, 7).start()
-
-        other_chips(to_chip)
+        def to_chip(k, carry):
+            q = lax.rem(k, NY) * NZ + lax.div(k, NY)
+
+            @pl.when(q != chip)
+            def _():
+                for c in (1, 0):
+                    tile_copy(c3.at[mine], c3.at[mine], 2 * q + c, 6, 7).start()
+
+            return carry
+
+        lax.fori_loop(0, NY * NZ, to_chip, 0)
         tile_copy(c3.at[mine], c3.at[mine], 2 * chip + 1 - core, 6, 7).start()
 
     c_dira.wait_recv()
@@ -371,7 +382,7 @@
             *[vm((tok, half), BF16)] * 8,
             dma((4,)), dma((nb,)),
             dma((3,)), dma((3,)), dma((3,)), dma((3,)), dma((3,)), dma((3,)),
-            dma((8,)), dma((6,)), dma((6,)),
+            dma((8,)), dma((6,)), dma((6,)), pltpu.SemaphoreType.REGULAR,
         ],
         compiler_params=pltpu.CompilerParams(
             collective_id=0, has_side_effects=True, vmem_limit_bytes=60 * 2**20

time: 56.6 us -> 54.5 us (0.963)
  Pallas kernels: 55.9 us -> 53.8 us
    pallas_call x1, Pallas kernels: 55 us -> 52.9 us  [local(): pl.pallas_call(functools.partial(kernel, scale), out_shape=(vm((tok, widt...]
where the time goes in v3:
time: 54.5 us; the launch traced here: 54.4 us
  Pallas kernels  53.8 us (99%)
  between operations  0.64 us (1%)
    pallas_call x1, Pallas kernels, local(): pl.pallas_call(functools.partial(kernel, scale), out_shape=(vm((tok, widt...  52.9 us

profile of v3, /device:TPU:1, one launch (start us, length us, event | category | flops | bytes accessed | tf_op | source)
XLA Modules:
  0.0 54.4 jit_solution(11214711740396091183)
XLA Ops:
  0.6 52.9 %shard_map.67 = (bf16[64,4096]{1,0:T(8,128)(2,1)S(1)}, f32[32,1024]{1,0:T(8,128)S(1)}, f32[32,1280]{1,0:T(8,128)S(1)}) custom-call(bf16[64,4096]{1,0:T(8,128)(2,1)} %x_ref.1, bf16[256,1280]{1,0:T(8,128)(2,1)} %g_ref.1, bf16[4096,1280]{1,0:T(8,128)(2,1)} %w_ref.1, f32[32,1280]{1,0:T(8,128)} %bitcast.3), custom_call_target="tpu_custom_call" | custom-call | tf_op jit(solution)/shard_map/pallas_call | solution.py:366
  53.5 0.9 %shard_map.68 = (bf16[64,4096]{1,0:T(8,128)(2,1)}, f32[32,1024]{1,0:T(8,128)}, f32[32,1280]{1,0:T(8,128)}) custom-call(bf16[64,4096]{1,0:T(8,128)(2,1)S(1)} %get-tuple-element.9.a, f32[32,1024]{1,0:T(8,128)S(1)} %get-tuple-element.10.b, f32[32,1280]{1,0:T(8,128)S(1)} %get-tuple-element.11.c), custom_call_target="tpu_custom_call" | custom-call | tf_op jit(solution)/shard_map/pallas_call | solution.py:391

commit v4 on v3

--- a/solution.py
+++ b/solution.py
@@ -48,18 +48,14 @@
     return m[:, n : 2 * n] / jnp.sqrt(diag)
 
 
-def far_offset(j, half):
-    return half + lax.div(j + 1, 2) * (1 - 2 * lax.rem(j, 2))
-
-
 def kernel(
     scale,
     x_ref, g_ref, w_ref, q_ref,
     igo, bas, cof,
-    xv, gv, qv, wv, xs, yr, fp, r2, f3, zr, cp, r4, c3,
+    xv, gv, qv, wv, xs, yr, fp, hp, r2, f3, zr, cp, hc, r4, r5, c3,
     igp, dira, dirb, rela, relb, suma, sumb, fina, finb,
     lsem, wsem, ysem_s, ysem_r, xsem_s, xsem_r, zsem_s, zsem_r,
-    rsem, isem_s, isem_r, far_sem,
+    rsem, bsem, isem_s, isem_r, far_sem,
 ):
     d = lax.axis_index("dp")
     t = lax.axis_index("tensor")
@@ -71,15 +67,6 @@
     share = xs.shape[2]
     half = igp.shape[1] // 2
     left, right, across = lax.rem(t + 3, nt), lax.rem(t + 1, nt), lax.rem(t + 2, nt)
-
-    def other_chips(fn):
-        def body(k, carry):
-            qy = lax.rem(cy + far_offset(lax.rem(k, NY), NY // 2), NY)
-            qz = lax.rem(cz + far_offset(lax.div(k, NY), NZ // 2), NZ)
-            fn(qy * NZ + qz)
-            return carry
-
-        lax.fori_loop(0, NY * NZ - 1, body, 0)
 
     bar = pltpu.get_barrier_semaphore()
 
@@ -170,18 +157,50 @@
 
     def tile_copy(src, dst, dp, s, r):
         return pltpu.make_async_remote_copy(
-            src_ref=src, dst_ref=dst, send_sem=rsem.at[s], recv_sem=rsem.at[r],
+            src_ref=src, dst_ref=dst, send_sem=rsem.at[s], recv_sem=bsem.at[r],
             device_id=(dp, t), device_id_type=MESH)
 
-    def slot(to):
-        return lax.rem(d - to + 127, 64)
+    oys = [lax.rem(cy + dy, NY) for dy in range(NY)]
+    ozs = [lax.rem(cz + dz, NZ) for dz in range(NZ)]
+    dev_y = [oy * (2 * NZ) + core for oy in oys]
+    dev_z = [2 * oz for oz in ozs]
+    tile_y = [lax.rem(oy, 2) * NZ for oy in oys]
+    turn_y = [lax.div(oy, 2) for oy in oys]
+    turn_z = [lax.rem(oz + NZ // 2, NZ) - oz for oz in ozs]
+    more_z = [lax.rem(oz, 4) == 2 for oz in ozs]
+
+    def device(dy, dz):
+        return dev_y[dy] + dev_z[dz]
+
+    def tile_of(dy, dz):
+        return tile_y[dy] + ozs[dz] + turn_y[dy] * turn_z[dz]
+
+    def more_of(dy, dz):
+        return 16 + lax.div(tile_of(dy, dz), 4)
+
+    far_first = [(dy, dz) for dz in (4, 3, 5, 2, 6, 1, 7, 0) for dy in (2, 1, 3, 0) if dy or dz]
+
+    served = [(dy, dz) for dz in (2, 6, 1, 7, 0) for dy in (2, 1, 3, 0)
+              if dz in (1, 7) or (dz == 2 and dy != 2) or (dz == 6 and dy == 0) or (dz == 0 and dy)]
+
+    last = NY * NZ - 1
+    sibling = 2 * chip + 1 - core
+    other_core = 1 - 2 * core
+    own_tile = tile_of(0, 0)
+    n1, n2 = fp.shape[0] // 2, cp.shape[0] // 2
+
+    swap_f = tile_copy(fp.at[pl.ds((1 - core) * n1, n1)], hp, sibling, 0, 0)
+    swap_f.start()
+    swap_f.wait_recv()
+    half_f = pl.ds(core * n1, n1)
+    fp[half_f] = fp[half_f] + hp[...]
 
     pl.semaphore_wait(far_sem, len(z_line))
-    other_chips(lambda q: tile_copy(fp.at[q], r2.at[slot(2 * q)], 2 * q, 0, 1).start())
-
-    @pl.when(core == 1)
-    def _():
-        tile_copy(fp.at[chip], r2.at[slot(2 * chip)], 2 * chip, 0, 1).start()
+    base_f = core * n1
+    for dy, dz in far_first:
+        tile_copy(fp.at[base_f + tile_of(dy, dz)], r2.at[chip], device(dy, dz), 1, 1).start()
+    mine_f = base_f + own_tile
+    r2[chip] = fp[mine_f]
 
     def rows_of(o):
         return pl.ds(pl.multiple_of(o * tok, tok), tok)
@@ -199,26 +218,16 @@
     for c in (c_rela, c_relb, c_dira, c_dirb):
         c.start()
 
-    @pl.when(core == 0)
-    def _():
-        r2[63] = fp[chip]
-        wait_tiles(r2, 63, rsem.at[1])
-        f3[chip] = jnp.sum(r2[...], axis=0)
-
-        def to_chip(q):
-            for c in range(2):
-                tile_copy(f3.at[chip], f3.at[chip], 2 * q + c, 2, 3).start()
-
-        other_chips(to_chip)
-        tile_copy(f3.at[chip], f3.at[chip], 2 * chip + 1, 2, 3).start()
-
-    @pl.when(core == 0)
-    def _():
-        wait_tiles(f3, 31, rsem.at[3])
-
-    @pl.when(core == 1)
-    def _():
-        wait_tiles(f3, 32, rsem.at[3])
+    wait_tiles(r2, last, bsem.at[1])
+    f3[mine_f] = jnp.sum(r2[...], axis=0)
+    def broadcast(ref, tile, s, r):
+        for dy, dz in served:
+            for other in (device(dy, dz), device(dy, dz) + other_core):
+                tile_copy(ref.at[tile], ref.at[tile], other, s, r).start()
+        tile_copy(ref.at[tile], ref.at[tile], sibling, s, r).start()
+
+    broadcast(f3, mine_f, 2, 2)
+    wait_tiles(f3, 31, bsem.at[2])
 
     ft = jnp.concatenate(
         [jnp.concatenate([f3[i * ncol + j] for j in range(ncol)], axis=1) for i in range(R // 8)], axis=0
@@ -242,30 +251,30 @@
 
     cpart = fdot(zt, gv[...], NN)
     ncc = cpart.shape[1] // 128
-    nct = R // 8 * ncc
     for i in range(R // 8):
         for j in range(ncc):
             cp[i * ncc + j] = cpart[8 * i : 8 * i + 8, 128 * j : 128 * j + 128]
-    other_chips(lambda q: tile_copy(cp.at[q], r4.at[slot(2 * q)], 2 * q, 4, 5).start())
-
-    @pl.when(core == 1)
-    def _():
-        tile_copy(cp.at[chip], r4.at[slot(2 * chip)], 2 * chip, 4, 5).start()
-
-    @pl.when(core == 0)
-    def _():
-        r4[63] = cp[chip]
-
-    for e in range(nct - 32):
-        to = 8 * e + 1
-
-        @pl.when(d != to)
+    swap_c = tile_copy(cp.at[pl.ds((1 - core) * n2, n2)], hc, sibling, 3, 3)
+    swap_c.start()
+    swap_c.wait_recv()
+    half_c = pl.ds(core * n2, n2)
+    cp[half_c] = cp[half_c] + hc[...]
+
+    base_c = core * n2
+    for dy, dz in far_first:
+        tile_copy(cp.at[base_c + tile_of(dy, dz)], r4.at[chip], device(dy, dz), 4, 4).start()
+    for z in range(NZ):
+
+        @pl.when(more_z[z])
         def _():
-            tile_copy(cp.at[32 + e], r4.at[slot(to)], to, 4, 5).start()
-
-        @pl.when(d == to)
-        def _():
-            r4[63] = cp[32 + e]
+            for dy, dz in far_first:
+                if dz == z:
+                    tile_copy(cp.at[base_c + more_of(dy, dz)], r5.at[chip], device(dy, dz), 7, 6).start()
+
+    more = more_z[0]
+    mine = base_c + own_tile
+    mine_more = base_c + more_of(0, 0)
+    r4[chip] = cp[mine]
 
     c_rela.wait_recv()
     suma[...] = (rela[...].astype(F32) + igp[rows_of(left), ca].astype(F32)).astype(BF16)
@@ -279,26 +288,16 @@
     linv = inverse_cholesky(gram)
     bas[...] = lax.dot_general(linv, ft, NN, precision=HIGH, preferred_element_type=F32)
 
-    owner = jnp.logical_or(core == 0, lax.rem(chip, 4) == 0)
-    mine = chip * (1 - core) + (32 + lax.div(chip, 4)) * core
-
-    @pl.when(owner)
+    wait_tiles(r4, last, bsem.at[4])
+    c3[mine] = jnp.sum(r4[...], axis=0)
+    broadcast(c3, mine, 5, 5)
+
+    @pl.when(more)
     def _():
-        wait_tiles(r4, 63, rsem.at[5])
-        c3[mine] = jnp.sum(r4[...], axis=0)
-
-        def to_chip(k, carry):
-            q = lax.rem(k, NY) * NZ + lax.div(k, NY)
-
-            @pl.when(q != chip)
-            def _():
-                for c in (1, 0):
-                    tile_copy(c3.at[mine], c3.at[mine], 2 * q + c, 6, 7).start()
-
-            return carry
-
-        lax.fori_loop(0, NY * NZ, to_chip, 0)
-        tile_copy(c3.at[mine], c3.at[mine], 2 * chip + 1 - core, 6, 7).start()
+        r5[chip] = cp[mine_more]
+        wait_tiles(r5, last, bsem.at[6])
+        c3[mine_more] = jnp.sum(r5[...], axis=0)
+        broadcast(c3, mine_more, 6, 5)
 
     c_dira.wait_recv()
     c_fina.wait_recv()
@@ -307,13 +306,13 @@
     c_finb.wait_recv()
     igo[:, cb] = (igp[rows_of(t), cb].astype(F32) + dirb[...].astype(F32) + finb[...].astype(F32)).astype(BF16)
 
-    @pl.when(owner)
+    @pl.when(more)
     def _():
-        wait_tiles(c3, nct - 1, rsem.at[7])
-
-    @pl.when(jnp.logical_not(owner))
+        wait_tiles(c3, 2 * n2 - 2, bsem.at[5])
+
+    @pl.when(jnp.logical_not(more))
     def _():
-        wait_tiles(c3, nct, rsem.at[7])
+        wait_tiles(c3, 2 * n2 - 1, bsem.at[5])
 
     ct = jnp.concatenate(
         [jnp.concatenate([c3[i * ncc + j] for j in range(ncc)], axis=1) for i in range(R // 8)], axis=0
@@ -322,24 +321,21 @@
 
     for c in ycopies + xcopies + zcopies + [c_rela, c_relb, c_dira, c_dirb, c_fina, c_finb]:
         c.wait_send()
-
-    @pl.when(core == 0)
+    swap_f.wait_send()
+    swap_c.wait_send()
+    wait_tiles(f3, 31, rsem.at[1])
+    wait_tiles(f3, 31, rsem.at[2])
+    wait_tiles(f3, 31, rsem.at[4])
+    wait_tiles(f3, 31, rsem.at[5])
+
+    @pl.when(more)
     def _():
-        wait_tiles(r2, 31, rsem.at[0])
-        wait_tiles(r2, 63, rsem.at[2])
-
-    @pl.when(core == 1)
+        wait_tiles(f3, 31, rsem.at[6])
+        wait_tiles(f3, 7, rsem.at[7])
+
+    @pl.when(jnp.logical_not(more))
     def _():
-        wait_tiles(r2, 32, rsem.at[0])
-
-    @pl.when(owner)
-    def _():
-        wait_tiles(r4, nct - 1, rsem.at[4])
-        wait_tiles(r4, 63, rsem.at[6])
-
-    @pl.when(jnp.logical_not(owner))
-    def _():
-        wait_tiles(r4, nct, rsem.at[4])
+        wait_tiles(f3, 8, rsem.at[7])
 
 
 def write_out(a, b, c, ao, bo, co, sem):
@@ -375,14 +371,15 @@
         scratch_shapes=[
             vm((tok, width), BF16), vm((rows, hid), BF16), vm((R, hid), F32), vm((width, hid), BF16),
             vm((nt, tok, share), BF16), vm((nt, R, rows), F32),
-            vm((32, 8, 128), F32), vm((64, 8, 128), F32), vm((32, 8, 128), F32),
+            vm((32, 8, 128), F32), vm((16, 8, 128), F32), vm((32, 8, 128), F32), vm((32, 8, 128), F32),
             vm((nt, R, rows + 128), F32),
-            vm((40, 8, 128), F32), vm((64, 8, 128), F32), vm((40, 8, 128), F32),
+            vm((40, 8, 128), F32), vm((20, 8, 128), F32), vm((32, 8, 128), F32), vm((32, 8, 128), F32),
+            vm((40, 8, 128), F32),
             vm((rows, width), BF16),
             *[vm((tok, half), BF16)] * 8,
             dma((4,)), dma((nb,)),
             dma((3,)), dma((3,)), dma((3,)), dma((3,)), dma((3,)), dma((3,)),
-            dma((8,)), dma((6,)), dma((6,)), pltpu.SemaphoreType.REGULAR,
+            dma((8,)), dma((7,)), dma((6,)), dma((6,)), pltpu.SemaphoreType.REGULAR,
         ],
         compiler_params=pltpu.CompilerParams(
             collective_id=0, has_side_effects=True, vmem_limit_bytes=60 * 2**20

time: 54.5 us -> 53.9 us (0.989)
  Pallas kernels: 53.8 us -> 53.2 us
    pallas_call x1, Pallas kernels: 52.9 us -> 52.3 us  [local(): pl.pallas_call(functools.partial(kernel, scale), out_shape=(vm((tok, widt...]
where the time goes in v4:
time: 53.9 us; the launch traced here: 53.8 us
  Pallas kernels  53.2 us (99%)
  between operations  0.64 us (1%)
    pallas_call x1, Pallas kernels, local(): pl.pallas_call(functools.partial(kernel, scale), out_shape=(vm((tok, widt...  52.3 us

profile of v4, /device:TPU:1, one launch (start us, length us, event | category | flops | bytes accessed | tf_op | source)
XLA Modules:
  0.0 53.8 jit_solution(10199021170670045885)
XLA Ops:
  0.6 52.3 %shard_map.67 = (bf16[64,4096]{1,0:T(8,128)(2,1)S(1)}, f32[32,1024]{1,0:T(8,128)S(1)}, f32[32,1280]{1,0:T(8,128)S(1)}) custom-call(bf16[64,4096]{1,0:T(8,128)(2,1)} %x_ref.1, bf16[256,1280]{1,0:T(8,128)(2,1)} %g_ref.1, bf16[4096,1280]{1,0:T(8,128)(2,1)} %w_ref.1, f32[32,1280]{1,0:T(8,128)} %bitcast.3), custom_call_target="tpu_custom_call" | custom-call | tf_op jit(solution)/shard_map/pallas_call | solution.py:362
  52.9 0.9 %shard_map.68 = (bf16[64,4096]{1,0:T(8,128)(2,1)}, f32[32,1024]{1,0:T(8,128)}, f32[32,1280]{1,0:T(8,128)}) custom-call(bf16[64,4096]{1,0:T(8,128)(2,1)S(1)} %get-tuple-element.9.a, f32[32,1024]{1,0:T(8,128)S(1)} %get-tuple-element.10.b, f32[32,1280]{1,0:T(8,128)S(1)} %get-tuple-element.11.c), custom_call_target="tpu_custom_call" | custom-call | tf_op jit(solution)/shard_map/pallas_call | solution.py:388

commit v5 on v4

--- a/solution.py
+++ b/solution.py
@@ -26,8 +26,8 @@
     return jnp.concatenate([hi, mid, low], axis=0)
 
 
-def fdot(a, b, dims):
-    r = lax.dot_general(split3(a), b, dims, preferred_element_type=F32)
+def fdot(pieces, b, dims):
+    r = lax.dot_general(pieces, b, dims, preferred_element_type=F32)
     return r[0:R] + r[R : 2 * R] + r[2 * R : 3 * R]
 
 
@@ -52,9 +52,9 @@
     scale,
     x_ref, g_ref, w_ref, q_ref,
     igo, bas, cof,
-    xv, gv, qv, wv, xs, yr, fp, hp, r2, f3, zr, cp, hc, r4, r5, c3,
+    xv, gv, qv, wv, xs, yp, yr, yf, fp, hp, r2, f3, zr, gr, cp, hc, r4, c3,
     igp, dira, dirb, rela, relb, suma, sumb, fina, finb,
-    lsem, wsem, ysem_s, ysem_r, xsem_s, xsem_r, zsem_s, zsem_r,
+    lsem, wsem, ysem_s, ysem_r, xsem_s, xsem_r, zsem_s, zsem_r, gsem_s, gsem_r, fsem_s, fsem_r,
     rsem, bsem, isem_s, isem_r, far_sem,
 ):
     d = lax.axis_index("dp")
@@ -78,10 +78,10 @@
 
     z_line = [dp_index(0, dz, 0) for dz in (4, 3, 5, 2, 6, 1, 7)]
     group = [dp_index(dy, 0, dc) for dy in (2, 1, 3, 0) for dc in range(2) if dy or dc]
+    for k in range(1, nt):
+        greet(d, lax.rem(t + k, nt))
     for other in z_line + group:
         greet(other, t)
-    for k in range(1, nt):
-        greet(d, lax.rem(t + k, nt))
 
     loads = [
         pltpu.make_async_copy(q_ref, qv, lsem.at[0]),
@@ -105,7 +105,13 @@
 
     loads[0].wait()
     loads[1].wait()
-    yr[t] = fdot(qv[...], gv[...], NT)
+    yp[...] = fdot(split3(qv[...]), gv[...], NT)
+    ranks = R // nt
+
+    def ranks_of(o):
+        return pl.ds(pl.multiple_of(o * ranks, ranks), ranks)
+
+    yr[t] = yp[ranks_of(t)]
 
     loads[2].wait()
 
@@ -115,7 +121,7 @@
     for k in range(1, nt):
         to = lax.rem(t + k, nt)
         ycopies.append(pltpu.make_async_remote_copy(
-            src_ref=yr.at[t], dst_ref=yr.at[t], send_sem=ysem_s.at[k - 1], recv_sem=ysem_r.at[k - 1],
+            src_ref=yp.at[ranks_of(to)], dst_ref=yr.at[t], send_sem=ysem_s.at[k - 1], recv_sem=ysem_r.at[k - 1],
             device_id=(d, to), device_id_type=MESH))
         xcopies.append(pltpu.make_async_remote_copy(
             src_ref=xv.at[:, pl.ds(pl.multiple_of(to * share, share), share)], dst_ref=xs.at[t],
@@ -135,21 +141,25 @@
         igp[:, rows] = lax.dot_general(gv[...], wv[rows, :], NT, preferred_element_type=F32).astype(BF16)
         return carry
 
-    lax.fori_loop(0, nb, ig_block, 0)
-
+    lax.fori_loop(0, nb // 2, ig_block, 0)
     for c in ycopies:
         c.wait_recv()
-    yt = (yr[0] + yr[1]) + (yr[2] + yr[3])
+    yf[t] = (yr[0] + yr[1]) + (yr[2] + yr[3])
+    fcopies = []
+    for k in range(1, nt):
+        fcopies.append(pltpu.make_async_remote_copy(
+            src_ref=yf.at[t], dst_ref=yf.at[t], send_sem=fsem_s.at[k - 1], recv_sem=fsem_r.at[k - 1],
+            device_id=(d, lax.rem(t + k, nt)), device_id_type=MESH))
+    for c in fcopies:
+        c.start()
+    lax.fori_loop(nb // 2, nb, ig_block, 0)
+
+    for c in fcopies:
+        c.wait_recv()
+    yt = yf[...].reshape(R, nt * tok)
     for c in xcopies:
         c.wait_recv()
     loads[3].wait()
-
-    xsl = xs[...].reshape(nt * tok, share)
-    part = fdot(yt, xsl, NN) * scale
-    ncol = share // 128
-    for i in range(R // 8):
-        for j in range(ncol):
-            fp[i * ncol + j] = part[8 * i : 8 * i + 8, 128 * j : 128 * j + 128]
 
     def wait_tiles(ref, n, sem):
         view = ref.at[pl.ds(0, n)]
@@ -167,7 +177,6 @@
     tile_y = [lax.rem(oy, 2) * NZ for oy in oys]
     turn_y = [lax.div(oy, 2) for oy in oys]
     turn_z = [lax.rem(oz + NZ // 2, NZ) - oz for oz in ozs]
-    more_z = [lax.rem(oz, 4) == 2 for oz in ozs]
 
     def device(dy, dz):
         return dev_y[dy] + dev_z[dz]
@@ -175,32 +184,42 @@
     def tile_of(dy, dz):
         return tile_y[dy] + ozs[dz] + turn_y[dy] * turn_z[dz]
 
-    def more_of(dy, dz):
-        return 16 + lax.div(tile_of(dy, dz), 4)
-
     far_first = [(dy, dz) for dz in (4, 3, 5, 2, 6, 1, 7, 0) for dy in (2, 1, 3, 0) if dy or dz]
 
     served = [(dy, dz) for dz in (2, 6, 1, 7, 0) for dy in (2, 1, 3, 0)
               if dz in (1, 7) or (dz == 2 and dy != 2) or (dz == 6 and dy == 0) or (dz == 0 and dy)]
 
     last = NY * NZ - 1
+    pieces = fp.shape[0] // 2
+    ys = split3(yt)
+    width_f = share // 2
     sibling = 2 * chip + 1 - core
     other_core = 1 - 2 * core
     own_tile = tile_of(0, 0)
-    n1, n2 = fp.shape[0] // 2, cp.shape[0] // 2
-
-    swap_f = tile_copy(fp.at[pl.ds((1 - core) * n1, n1)], hp, sibling, 0, 0)
+
+    def factor_half(h):
+        columns = pl.ds(pl.multiple_of(h * width_f, width_f), width_f)
+        part = fdot(ys, xs[:, :, columns].reshape(nt * tok, width_f), NN) * scale
+        for k in range(pieces):
+            i, j = k % 4, k // 4
+            fp[h * pieces + k] = part[8 * i : 8 * i + 8, 128 * j : 128 * j + 128]
+
+    def half_of(h):
+        return pl.ds(h * pieces, pieces)
+
+    factor_half(1 - core)
+    swap_f = tile_copy(fp.at[half_of(1 - core)], hp, sibling, 0, 0)
     swap_f.start()
+    factor_half(core)
     swap_f.wait_recv()
-    half_f = pl.ds(core * n1, n1)
-    fp[half_f] = fp[half_f] + hp[...]
+    fp[half_of(core)] = fp[half_of(core)] + hp[...]
 
     pl.semaphore_wait(far_sem, len(z_line))
-    base_f = core * n1
+    base = core * pieces
     for dy, dz in far_first:
-        tile_copy(fp.at[base_f + tile_of(dy, dz)], r2.at[chip], device(dy, dz), 1, 1).start()
-    mine_f = base_f + own_tile
-    r2[chip] = fp[mine_f]
+        tile_copy(fp.at[base + tile_of(dy, dz)], r2.at[chip], device(dy, dz), 1, 1).start()
+    mine = base + own_tile
+    r2[chip] = fp[mine]
 
     def rows_of(o):
         return pl.ds(pl.multiple_of(o * tok, tok), tok)
@@ -219,61 +238,60 @@
         c.start()
 
     wait_tiles(r2, last, bsem.at[1])
-    f3[mine_f] = jnp.sum(r2[...], axis=0)
+    f3[mine] = jnp.sum(r2[...], axis=0)
     def broadcast(ref, tile, s, r):
         for dy, dz in served:
             for other in (device(dy, dz), device(dy, dz) + other_core):
                 tile_copy(ref.at[tile], ref.at[tile], other, s, r).start()
         tile_copy(ref.at[tile], ref.at[tile], sibling, s, r).start()
 
-    broadcast(f3, mine_f, 2, 2)
+    broadcast(f3, mine, 2, 2)
     wait_tiles(f3, 31, bsem.at[2])
 
     ft = jnp.concatenate(
-        [jnp.concatenate([f3[i * ncol + j] for j in range(ncol)], axis=1) for i in range(R // 8)], axis=0
+        [jnp.concatenate([f3[4 * j + i] for j in range(share // 128)], axis=1) for i in range(4)], axis=0
     )
-
-    zw = nt * tok
-    zr[t, :, 0:zw] = fdot(ft, xsl, NT) * scale
-    zr[t, :, zw : zw + R] = lax.dot_general(ft, ft, NT, precision=HIGH, preferred_element_type=F32)
-    zcopies = []
+    xsl = xs[...].reshape(nt * tok, share)
+
+    zr[t] = fdot(split3(ft), xsl, NT) * scale
+    zcopies, gcopies = [], []
     for k in range(1, nt):
         zcopies.append(pltpu.make_async_remote_copy(
             src_ref=zr.at[t], dst_ref=zr.at[t], send_sem=zsem_s.at[k - 1], recv_sem=zsem_r.at[k - 1],
             device_id=(d, lax.rem(t + k, nt)), device_id_type=MESH))
     for c in zcopies:
         c.start()
+    gr[t, :, 0:R] = lax.dot_general(ft, ft, NT, precision=HIGH, preferred_element_type=F32)
+    for k in range(1, nt):
+        gcopies.append(pltpu.make_async_remote_copy(
+            src_ref=gr.at[t], dst_ref=gr.at[t], send_sem=gsem_s.at[k - 1], recv_sem=gsem_r.at[k - 1],
+            device_id=(d, lax.rem(t + k, nt)), device_id_type=MESH))
+    for c in gcopies:
+        c.start()
     for c in zcopies:
         c.wait_recv()
-    zt = (zr[0, :, 0:zw] + zr[1, :, 0:zw]) + (zr[2, :, 0:zw] + zr[3, :, 0:zw])
-    gs = slice(zw, zw + R)
-    gram = (zr[0, :, gs] + zr[1, :, gs]) + (zr[2, :, gs] + zr[3, :, gs])
-
-    cpart = fdot(zt, gv[...], NN)
-    ncc = cpart.shape[1] // 128
-    for i in range(R // 8):
-        for j in range(ncc):
-            cp[i * ncc + j] = cpart[8 * i : 8 * i + 8, 128 * j : 128 * j + 128]
-    swap_c = tile_copy(cp.at[pl.ds((1 - core) * n2, n2)], hc, sibling, 3, 3)
+    zt = (zr[0] + zr[1]) + (zr[2] + zr[3])
+
+    zs = split3(zt)
+    width_c = gv.shape[1] // 2
+    edge_c = width_c - 128
+
+    def coeff_half(h):
+        columns = pl.ds(pl.multiple_of(h * width_c, 128), width_c)
+        part = fdot(zs, gv[:, columns], NN)
+        for k in range(pieces):
+            i, j = k % 4, k // 4
+            cp[h * pieces + k, 0:8] = part[8 * i : 8 * i + 8, 128 * j : 128 * j + 128]
+            cp[h * pieces + k, 8:10] = part[2 * k : 2 * k + 2, edge_c:width_c]
+
+    coeff_half(1 - core)
+    swap_c = tile_copy(cp.at[half_of(1 - core)], hc, sibling, 3, 3)
     swap_c.start()
+    coeff_half(core)
     swap_c.wait_recv()
-    half_c = pl.ds(core * n2, n2)
-    cp[half_c] = cp[half_c] + hc[...]
-
-    base_c = core * n2
+    cp[half_of(core)] = cp[half_of(core)] + hc[...]
     for dy, dz in far_first:
-        tile_copy(cp.at[base_c + tile_of(dy, dz)], r4.at[chip], device(dy, dz), 4, 4).start()
-    for z in range(NZ):
-
-        @pl.when(more_z[z])
-        def _():
-            for dy, dz in far_first:
-                if dz == z:
-                    tile_copy(cp.at[base_c + more_of(dy, dz)], r5.at[chip], device(dy, dz), 7, 6).start()
-
-    more = more_z[0]
-    mine = base_c + own_tile
-    mine_more = base_c + more_of(0, 0)
+        tile_copy(cp.at[base + tile_of(dy, dz)], r4.at[chip], device(dy, dz), 4, 4).start()
     r4[chip] = cp[mine]
 
     c_rela.wait_recv()
@@ -285,19 +303,16 @@
     c_finb = ig_copy(5, sumb, finb, right)
     c_finb.start()
 
+    for c in gcopies:
+        c.wait_recv()
+    gs = slice(0, R)
+    gram = (gr[0, :, gs] + gr[1, :, gs]) + (gr[2, :, gs] + gr[3, :, gs])
     linv = inverse_cholesky(gram)
     bas[...] = lax.dot_general(linv, ft, NN, precision=HIGH, preferred_element_type=F32)
 
     wait_tiles(r4, last, bsem.at[4])
     c3[mine] = jnp.sum(r4[...], axis=0)
     broadcast(c3, mine, 5, 5)
-
-    @pl.when(more)
-    def _():
-        r5[chip] = cp[mine_more]
-        wait_tiles(r5, last, bsem.at[6])
-        c3[mine_more] = jnp.sum(r5[...], axis=0)
-        broadcast(c3, mine_more, 6, 5)
 
     c_dira.wait_recv()
     c_fina.wait_recv()
@@ -306,36 +321,23 @@
     c_finb.wait_recv()
     igo[:, cb] = (igp[rows_of(t), cb].astype(F32) + dirb[...].astype(F32) + finb[...].astype(F32)).astype(BF16)
 
-    @pl.when(more)
-    def _():
-        wait_tiles(c3, 2 * n2 - 2, bsem.at[5])
-
-    @pl.when(jnp.logical_not(more))
-    def _():
-        wait_tiles(c3, 2 * n2 - 1, bsem.at[5])
-
-    ct = jnp.concatenate(
-        [jnp.concatenate([c3[i * ncc + j] for j in range(ncc)], axis=1) for i in range(R // 8)], axis=0
-    )
+    wait_tiles(c3, 31, bsem.at[5])
+    blocks = []
+    for h in range(2):
+        for j in range(4):
+            blocks.append(jnp.concatenate([c3[h * pieces + 4 * j + i, 0:8] for i in range(4)], axis=0))
+        blocks.append(jnp.concatenate([c3[h * pieces + k, 8:10] for k in range(pieces)], axis=0))
+    ct = jnp.concatenate(blocks, axis=1)
     cof[...] = lax.dot_general(linv, ct, NN, precision=HIGH, preferred_element_type=F32)
 
-    for c in ycopies + xcopies + zcopies + [c_rela, c_relb, c_dira, c_dirb, c_fina, c_finb]:
+    for c in ycopies + fcopies + xcopies + zcopies + gcopies + [c_rela, c_relb, c_dira, c_dirb, c_fina, c_finb]:
         c.wait_send()
     swap_f.wait_send()
     swap_c.wait_send()
     wait_tiles(f3, 31, rsem.at[1])
     wait_tiles(f3, 31, rsem.at[2])
-    wait_tiles(f3, 31, rsem.at[4])
-    wait_tiles(f3, 31, rsem.at[5])
-
-    @pl.when(more)
-    def _():
-        wait_tiles(f3, 31, rsem.at[6])
-        wait_tiles(f3, 7, rsem.at[7])
-
-    @pl.when(jnp.logical_not(more))
-    def _():
-        wait_tiles(f3, 8, rsem.at[7])
+    wait_tiles(c3, 31, rsem.at[4])
+    wait_tiles(c3, 31, rsem.at[5])
 
 
 def write_out(a, b, c, ao, bo, co, sem):
@@ -370,16 +372,15 @@
         out_specs=(vmem_spec,) * 3,
         scratch_shapes=[
             vm((tok, width), BF16), vm((rows, hid), BF16), vm((R, hid), F32), vm((width, hid), BF16),
-            vm((nt, tok, share), BF16), vm((nt, R, rows), F32),
+            vm((nt, tok, share), BF16), vm((R, rows), F32), *[vm((nt, R // nt, rows), F32)] * 2,
             vm((32, 8, 128), F32), vm((16, 8, 128), F32), vm((32, 8, 128), F32), vm((32, 8, 128), F32),
-            vm((nt, R, rows + 128), F32),
-            vm((40, 8, 128), F32), vm((20, 8, 128), F32), vm((32, 8, 128), F32), vm((32, 8, 128), F32),
-            vm((40, 8, 128), F32),
+            vm((nt, R, rows), F32), vm((nt, R, 128), F32),
+            vm((32, 10, 128), F32), vm((16, 10, 128), F32), vm((32, 10, 128), F32), vm((32, 10, 128), F32),
             vm((rows, width), BF16),
             *[vm((tok, half), BF16)] * 8,
             dma((4,)), dma((nb,)),
-            dma((3,)), dma((3,)), dma((3,)), dma((3,)), dma((3,)), dma((3,)),
-            dma((8,)), dma((7,)), dma((6,)), dma((6,)), pltpu.SemaphoreType.REGULAR,
+            *[dma((3,))] * 10,
+            dma((6,)), dma((6,)), dma((6,)), dma((6,)), pltpu.SemaphoreType.REGULAR,
         ],
         compiler_params=pltpu.CompilerParams(
             collective_id=0, has_side_effects=True, vmem_limit_bytes=60 * 2**20

time: 53.9 us -> 53 us (0.983)
  Pallas kernels: 53.2 us -> 52.3 us
    pallas_call x1, Pallas kernels: 52.3 us -> 51.4 us  [local(): pl.pallas_call(functools.partial(kernel, scale), out_shape=(vm((tok, widt...]
where the time goes in v5:
time: 53 us
  Pallas kernels  52.3 us (99%)
  between operations  0.64 us (1%)
    pallas_call x1, Pallas kernels, local(): pl.pallas_call(functools.partial(kernel, scale), out_shape=(vm((tok, widt...  51.4 us

profile of v5, /device:TPU:1, one launch (start us, length us, event | category | flops | bytes accessed | tf_op | source)
XLA Modules:
  0.0 53.0 jit_solution(8757618402272121510)
XLA Ops:
  0.6 51.4 %shard_map.67 = (bf16[64,4096]{1,0:T(8,128)(2,1)S(1)}, f32[32,1024]{1,0:T(8,128)S(1)}, f32[32,1280]{1,0:T(8,128)S(1)}) custom-call(bf16[64,4096]{1,0:T(8,128)(2,1)} %x_ref.1, bf16[256,1280]{1,0:T(8,128)(2,1)} %g_ref.1, bf16[4096,1280]{1,0:T(8,128)(2,1)} %w_ref.1, f32[32,1280]{1,0:T(8,128)} %bitcast.3), custom_call_target="tpu_custom_call" | custom-call | tf_op jit(solution)/shard_map/pallas_call | solution.py:364
  52.0 0.9 %shard_map.68 = (bf16[64,4096]{1,0:T(8,128)(2,1)}, f32[32,1024]{1,0:T(8,128)}, f32[32,1280]{1,0:T(8,128)}) custom-call(bf16[64,4096]{1,0:T(8,128)(2,1)S(1)} %get-tuple-element.9.a, f32[32,1024]{1,0:T(8,128)S(1)} %get-tuple-element.10.b, f32[32,1280]{1,0:T(8,128)S(1)} %get-tuple-element.11.c), custom_call_target="tpu_custom_call" | custom-call | tf_op jit(solution)/shard_map/pallas_call | solution.py:389

commit v6 on v5

--- a/solution.py
+++ b/solution.py
@@ -52,7 +52,7 @@
     scale,
     x_ref, g_ref, w_ref, q_ref,
     igo, bas, cof,
-    xv, gv, qv, wv, xs, yp, yr, yf, fp, hp, r2, f3, zr, gr, cp, hc, r4, c3,
+    xv, gv, qv, wv, xh, xz, yp, yr, yf, fp, r2, f3, zr, gr, cp, hc, r4, c3,
     igp, dira, dirb, rela, relb, suma, sumb, fina, finb,
     lsem, wsem, ysem_s, ysem_r, xsem_s, xsem_r, zsem_s, zsem_r, gsem_s, gsem_r, fsem_s, fsem_r,
     rsem, bsem, isem_s, isem_r, far_sem,
@@ -64,7 +64,8 @@
     cy, cz = lax.div(chip, NZ), lax.rem(chip, NZ)
     nt = 4
     tok = xv.shape[0]
-    share = xs.shape[2]
+    hw = xz.shape[3]
+    share = 2 * hw
     half = igp.shape[1] // 2
     left, right, across = lax.rem(t + 3, nt), lax.rem(t + 1, nt), lax.rem(t + 2, nt)
 
@@ -78,8 +79,10 @@
 
     z_line = [dp_index(0, dz, 0) for dz in (4, 3, 5, 2, 6, 1, 7)]
     group = [dp_index(dy, 0, dc) for dy in (2, 1, 3, 0) for dc in range(2) if dy or dc]
+    sibling = 2 * chip + 1 - core
     for k in range(1, nt):
         greet(d, lax.rem(t + k, nt))
+        greet(sibling, lax.rem(t + k, nt))
     for other in z_line + group:
         greet(other, t)
 
@@ -88,7 +91,7 @@
         pltpu.make_async_copy(g_ref, gv, lsem.at[1]),
         pltpu.make_async_copy(x_ref, xv, lsem.at[2]),
         pltpu.make_async_copy(
-            x_ref.at[:, pl.ds(pl.multiple_of(t * share, share), share)], xs.at[t], lsem.at[3]
+            x_ref.at[:, pl.ds(pl.multiple_of(t * share + core * hw, hw), hw)], xh.at[core, t], lsem.at[3]
         ),
     ]
     for c in loads:
@@ -115,7 +118,14 @@
 
     loads[2].wait()
 
-    pl.semaphore_wait(bar, len(z_line) + len(group) + nt - 1)
+    pl.semaphore_wait(bar, len(z_line) + len(group) + 2 * (nt - 1))
+
+    def x_copy(to, dc, n):
+        half = core + dc - 2 * core * dc
+        return pltpu.make_async_remote_copy(
+            src_ref=xv.at[:, pl.ds(pl.multiple_of(to * share + half * hw, hw), hw)], dst_ref=xh.at[core, t],
+            send_sem=xsem_s.at[n], recv_sem=xsem_r.at[n],
+            device_id=(d if dc == 0 else sibling, to), device_id_type=MESH)
 
     ycopies, xcopies = [], []
     for k in range(1, nt):
@@ -123,10 +133,9 @@
         ycopies.append(pltpu.make_async_remote_copy(
             src_ref=yp.at[ranks_of(to)], dst_ref=yr.at[t], send_sem=ysem_s.at[k - 1], recv_sem=ysem_r.at[k - 1],
             device_id=(d, to), device_id_type=MESH))
-        xcopies.append(pltpu.make_async_remote_copy(
-            src_ref=xv.at[:, pl.ds(pl.multiple_of(to * share, share), share)], dst_ref=xs.at[t],
-            send_sem=xsem_s.at[k - 1], recv_sem=xsem_r.at[k - 1],
-            device_id=(d, to), device_id_type=MESH))
+        for dc in range(2):
+            xcopies.append(x_copy(to, dc, 2 * k - 2 + dc))
+    xcopies.append(x_copy(t, 1, 6))
     for c in ycopies:
         c.start()
     for c in xcopies:
@@ -144,19 +153,22 @@
     lax.fori_loop(0, nb // 2, ig_block, 0)
     for c in ycopies:
         c.wait_recv()
-    yf[t] = (yr[0] + yr[1]) + (yr[2] + yr[3])
+    yf[core, t] = (yr[0] + yr[1]) + (yr[2] + yr[3])
     fcopies = []
-    for k in range(1, nt):
-        fcopies.append(pltpu.make_async_remote_copy(
-            src_ref=yf.at[t], dst_ref=yf.at[t], send_sem=fsem_s.at[k - 1], recv_sem=fsem_r.at[k - 1],
-            device_id=(d, lax.rem(t + k, nt)), device_id_type=MESH))
+    for k in range(nt):
+        for dc in range(2):
+            if k or dc:
+                fcopies.append(pltpu.make_async_remote_copy(
+                    src_ref=yf.at[core, t], dst_ref=yf.at[core, t],
+                    send_sem=fsem_s.at[2 * k + dc - 1], recv_sem=fsem_r.at[2 * k + dc - 1],
+                    device_id=(d if dc == 0 else sibling, lax.rem(t + k, nt)), device_id_type=MESH))
     for c in fcopies:
         c.start()
     lax.fori_loop(nb // 2, nb, ig_block, 0)
 
     for c in fcopies:
         c.wait_recv()
-    yt = yf[...].reshape(R, nt * tok)
+    yt = jnp.concatenate([yf[g].reshape(R, nt * tok) for g in range(2)], axis=1)
     for c in xcopies:
         c.wait_recv()
     loads[3].wait()
@@ -190,36 +202,31 @@
               if dz in (1, 7) or (dz == 2 and dy != 2) or (dz == 6 and dy == 0) or (dz == 0 and dy)]
 
     last = NY * NZ - 1
-    pieces = fp.shape[0] // 2
-    ys = split3(yt)
-    width_f = share // 2
-    sibling = 2 * chip + 1 - core
+    pieces = fp.shape[0]
     other_core = 1 - 2 * core
     own_tile = tile_of(0, 0)
 
-    def factor_half(h):
-        columns = pl.ds(pl.multiple_of(h * width_f, width_f), width_f)
-        part = fdot(ys, xs[:, :, columns].reshape(nt * tok, width_f), NN) * scale
-        for k in range(pieces):
-            i, j = k % 4, k // 4
-            fp[h * pieces + k] = part[8 * i : 8 * i + 8, 128 * j : 128 * j + 128]
+    part = fdot(split3(yt), xh[...].reshape(2 * nt * tok, hw), NN) * scale
+    for k in range(pieces):
+        i, j = k % 4, k // 4
+        fp[k] = part[8 * i : 8 * i + 8, 128 * j : 128 * j + 128]
 
     def half_of(h):
         return pl.ds(h * pieces, pieces)
-
-    factor_half(1 - core)
-    swap_f = tile_copy(fp.at[half_of(1 - core)], hp, sibling, 0, 0)
-    swap_f.start()
-    factor_half(core)
-    swap_f.wait_recv()
-    fp[half_of(core)] = fp[half_of(core)] + hp[...]
 
     pl.semaphore_wait(far_sem, len(z_line))
     base = core * pieces
     for dy, dz in far_first:
-        tile_copy(fp.at[base + tile_of(dy, dz)], r2.at[chip], device(dy, dz), 1, 1).start()
+        tile_copy(fp.at[tile_of(dy, dz)], r2.at[chip], device(dy, dz), 1, 1).start()
     mine = base + own_tile
-    r2[chip] = fp[mine]
+    r2[chip] = fp[own_tile]
+
+    x_swap = pltpu.make_async_remote_copy(
+        src_ref=xh.at[1 - core], dst_ref=xz.at[core], send_sem=xsem_s.at[7], recv_sem=xsem_r.at[7],
+        device_id=(sibling, t), device_id_type=MESH)
+    x_swap.start()
+    x_keep = pltpu.make_async_copy(xh.at[core], xz.at[core], lsem.at[4])
+    x_keep.start()
 
     def rows_of(o):
         return pl.ds(pl.multiple_of(o * tok, tok), tok)
@@ -248,12 +255,18 @@
     broadcast(f3, mine, 2, 2)
     wait_tiles(f3, 31, bsem.at[2])
 
-    ft = jnp.concatenate(
-        [jnp.concatenate([f3[4 * j + i] for j in range(share // 128)], axis=1) for i in range(4)], axis=0
-    )
-    xsl = xs[...].reshape(nt * tok, share)
-
-    zr[t] = fdot(split3(ft), xsl, NT) * scale
+    def columns(h):
+        return jnp.concatenate(
+            [jnp.concatenate([f3[h * pieces + 4 * j + i] for j in range(hw // 128)], axis=1) for i in range(4)], axis=0
+        )
+
+    x_keep.wait()
+    x_swap.wait_recv()
+    halves = [columns(0), columns(1)]
+    ft = jnp.concatenate(halves, axis=1)
+    z_parts = [fdot(split3(halves[h]), xz[h].reshape(nt * tok, hw), NT) for h in range(2)]
+
+    zr[t] = (z_parts[0] + z_parts[1]) * scale
     zcopies, gcopies = [], []
     for k in range(1, nt):
         zcopies.append(pltpu.make_async_remote_copy(
@@ -332,7 +345,7 @@
 
     for c in ycopies + fcopies + xcopies + zcopies + gcopies + [c_rela, c_relb, c_dira, c_dirb, c_fina, c_finb]:
         c.wait_send()
-    swap_f.wait_send()
+    x_swap.wait_send()
     swap_c.wait_send()
     wait_tiles(f3, 31, rsem.at[1])
     wait_tiles(f3, 31, rsem.at[2])
@@ -372,14 +385,15 @@
         out_specs=(vmem_spec,) * 3,
         scratch_shapes=[
             vm((tok, width), BF16), vm((rows, hid), BF16), vm((R, hid), F32), vm((width, hid), BF16),
-            vm((nt, tok, share), BF16), vm((R, rows), F32), *[vm((nt, R // nt, rows), F32)] * 2,
-            vm((32, 8, 128), F32), vm((16, 8, 128), F32), vm((32, 8, 128), F32), vm((32, 8, 128), F32),
+            *[vm((2, nt, tok, share // 2), BF16)] * 2,
+            vm((R, rows), F32), vm((nt, R // nt, rows), F32), vm((2, nt, R // nt, rows), F32),
+            vm((16, 8, 128), F32), vm((32, 8, 128), F32), vm((32, 8, 128), F32),
             vm((nt, R, rows), F32), vm((nt, R, 128), F32),
             vm((32, 10, 128), F32), vm((16, 10, 128), F32), vm((32, 10, 128), F32), vm((32, 10, 128), F32),
             vm((rows, width), BF16),
             *[vm((tok, half), BF16)] * 8,
-            dma((4,)), dma((nb,)),
-            *[dma((3,))] * 10,
+            dma((5,)), dma((nb,)),
+            *[dma((3,))] * 2, *[dma((8,))] * 2, *[dma((3,))] * 4, *[dma((7,))] * 2,
             dma((6,)), dma((6,)), dma((6,)), dma((6,)), pltpu.SemaphoreType.REGULAR,
         ],
         compiler_params=pltpu.CompilerParams(

time: 53 us -> 53 us (level)
  no operation moved by 1% of the time
where the time goes in v6:
time: 53 us; the launch traced here: 52.9 us
  Pallas kernels  52.3 us (99%)
  between operations  0.64 us (1%)
    pallas_call x1, Pallas kernels, local(): pl.pallas_call(functools.partial(kernel, scale), out_shape=(vm((tok, widt...  51.4 us

profile of v6, /device:TPU:1, one launch (start us, length us, event | category | flops | bytes accessed | tf_op | source)
XLA Modules:
  0.0 52.9 jit_solution(14983747087634980050)
XLA Ops:
  0.6 51.4 %shard_map.67 = (bf16[64,4096]{1,0:T(8,128)(2,1)S(1)}, f32[32,1024]{1,0:T(8,128)S(1)}, f32[32,1280]{1,0:T(8,128)S(1)}) custom-call(bf16[64,4096]{1,0:T(8,128)(2,1)} %x_ref.1, bf16[256,1280]{1,0:T(8,128)(2,1)} %g_ref.1, bf16[4096,1280]{1,0:T(8,128)(2,1)} %w_ref.1, f32[32,1280]{1,0:T(8,128)} %bitcast.3), custom_call_target="tpu_custom_call" | custom-call | tf_op jit(solution)/shard_map/pallas_call | solution.py:377
  52.0 0.9 %shard_map.68 = (bf16[64,4096]{1,0:T(8,128)(2,1)}, f32[32,1024]{1,0:T(8,128)}, f32[32,1280]{1,0:T(8,128)}) custom-call(bf16[64,4096]{1,0:T(8,128)(2,1)S(1)} %get-tuple-element.9.a, f32[32,1024]{1,0:T(8,128)S(1)} %get-tuple-element.10.b, f32[32,1280]{1,0:T(8,128)S(1)} %get-tuple-element.11.c), custom_call_target="tpu_custom_call" | custom-call | tf_op jit(solution)/shard_map/pallas_call | solution.py:403

commit v7 on v6

--- a/solution.py
+++ b/solution.py
@@ -80,7 +80,7 @@
     z_line = [dp_index(0, dz, 0) for dz in (4, 3, 5, 2, 6, 1, 7)]
     group = [dp_index(dy, 0, dc) for dy in (2, 1, 3, 0) for dc in range(2) if dy or dc]
     sibling = 2 * chip + 1 - core
-    for k in range(1, nt):
+    for k in (2, 1, 3):
         greet(d, lax.rem(t + k, nt))
         greet(sibling, lax.rem(t + k, nt))
     for other in z_line + group:
@@ -128,7 +128,7 @@
             device_id=(d if dc == 0 else sibling, to), device_id_type=MESH)
 
     ycopies, xcopies = [], []
-    for k in range(1, nt):
+    for k in (2, 1, 3):
         to = lax.rem(t + k, nt)
         ycopies.append(pltpu.make_async_remote_copy(
             src_ref=yp.at[ranks_of(to)], dst_ref=yr.at[t], send_sem=ysem_s.at[k - 1], recv_sem=ysem_r.at[k - 1],
@@ -155,7 +155,7 @@
         c.wait_recv()
     yf[core, t] = (yr[0] + yr[1]) + (yr[2] + yr[3])
     fcopies = []
-    for k in range(nt):
+    for k in (2, 1, 3, 0):
         for dc in range(2):
             if k or dc:
                 fcopies.append(pltpu.make_async_remote_copy(
@@ -268,14 +268,14 @@
 
     zr[t] = (z_parts[0] + z_parts[1]) * scale
     zcopies, gcopies = [], []
-    for k in range(1, nt):
+    for k in (2, 1, 3):
         zcopies.append(pltpu.make_async_remote_copy(
             src_ref=zr.at[t], dst_ref=zr.at[t], send_sem=zsem_s.at[k - 1], recv_sem=zsem_r.at[k - 1],
             device_id=(d, lax.rem(t + k, nt)), device_id_type=MESH))
     for c in zcopies:
         c.start()
     gr[t, :, 0:R] = lax.dot_general(ft, ft, NT, precision=HIGH, preferred_element_type=F32)
-    for k in range(1, nt):
+    for k in (2, 1, 3):
         gcopies.append(pltpu.make_async_remote_copy(
             src_ref=gr.at[t], dst_ref=gr.at[t], send_sem=gsem_s.at[k - 1], recv_sem=gsem_r.at[k - 1],
             device_id=(d, lax.rem(t + k, nt)), device_id_type=MESH))

time: 53 us -> 52.4 us (0.989)
  Pallas kernels: 52.3 us -> 51.7 us
    pallas_call x1, Pallas kernels: 51.4 us -> 50.8 us  [local(): pl.pallas_call(functools.partial(kernel, scale), out_shape=(vm((tok, widt...]
where the time goes in v7:
time: 52.4 us; the launch traced here: 52.3 us
  Pallas kernels  51.7 us (99%)
  between operations  0.64 us (1%)
    pallas_call x1, Pallas kernels, local(): pl.pallas_call(functools.partial(kernel, scale), out_shape=(vm((tok, widt...  50.8 us

profile of v7, /device:TPU:1, one launch (start us, length us, event | category | flops | bytes accessed | tf_op | source)
XLA Modules:
  0.0 52.3 jit_solution(1988266403120441576)
XLA Ops:
  0.6 50.8 %shard_map.67 = (bf16[64,4096]{1,0:T(8,128)(2,1)S(1)}, f32[32,1024]{1,0:T(8,128)S(1)}, f32[32,1280]{1,0:T(8,128)S(1)}) custom-call(bf16[64,4096]{1,0:T(8,128)(2,1)} %x_ref.1, bf16[256,1280]{1,0:T(8,128)(2,1)} %g_ref.1, bf16[4096,1280]{1,0:T(8,128)(2,1)} %w_ref.1, f32[32,1280]{1,0:T(8,128)} %bitcast.3), custom_call_target="tpu_custom_call" | custom-call | tf_op jit(solution)/shard_map/pallas_call | solution.py:377
  51.4 0.9 %shard_map.68 = (bf16[64,4096]{1,0:T(8,128)(2,1)}, f32[32,1024]{1,0:T(8,128)}, f32[32,1280]{1,0:T(8,128)}) custom-call(bf16[64,4096]{1,0:T(8,128)(2,1)S(1)} %get-tuple-element.9.a, f32[32,1024]{1,0:T(8,128)S(1)} %get-tuple-element.10.b, f32[32,1280]{1,0:T(8,128)S(1)} %get-tuple-element.11.c), custom_call_target="tpu_custom_call" | custom-call | tf_op jit(solution)/shard_map/pallas_call | solution.py:403
